TPU v7x, 32 devices: a whole 2x2x4 slice. The times are simulated.
32 devices in a mesh: sta: 8 (over y, x, core), win: 4 (over z).
Axes of the slice: x: 2, y: 2, z: 4, core: 2. Of those that a mesh axis runs over, the one named last changes fastest.
Arguments:
- traces: float32 [64, 64, 2048], P('sta', 'win'), may hold values from -24 to 24
- gap_mask: int32 [64, 64], P('sta', 'win'), may hold values 0 or 1
- pair_mask: int32 [64, 5, 8], P('sta'), may hold values from 0 to 1, as said below
Outputs:
- pws: float32 [64, 5, 8, 512], P('sta', None, None, 'win')
Inputs may be any that keep to these rules, and one draw needn't show every extreme that they name: pair_mask is 0 for a station paired with itself (offset index 2, same station of the block).
All inputs are finite; a program needn't handle non-finite values. No bound on the sum of `gap_mask` on one device may be relied on, other than what follows from the above.
Results may differ from a plain program's by a relative error of at most 0.0003.
Values may be sent and summed in bfloat16 or wider, within the bound.
No kernel may reach another device: no remote copies, remote signals or barrier semaphores. Data moves between devices by JAX's collectives and lax.ppermute only.
A program may use at most 128 MiB of HBM per device.

v0:
```python
import math

import jax
import jax.numpy as jnp
from jax import lax
from jax.sharding import PartitionSpec as P

SAMPLES = 2048
F = 1024
LAGS = 512
WBLK = 128
REACH = 2


def passed_along(block, axis, distance):
    devices = range(lax.axis_size(axis))
    route = [((i - distance) % len(devices), i) for i in devices]
    return lax.ppermute(block, axis, route)


def transform_table():
    moments = jnp.arange(SAMPLES, dtype=jnp.int32)
    frequency = jnp.arange(F, dtype=jnp.int32)
    product = moments[:, None] * frequency[None, :] % SAMPLES
    angle = product.astype(jnp.float32) * (2.0 * math.pi / SAMPLES)
    return jnp.concatenate([jnp.cos(angle), -jnp.sin(angle)], axis=1)


def inverse_table():
    frequency = jnp.arange(F, dtype=jnp.int32)
    delays = jnp.arange(LAGS, dtype=jnp.int32) - LAGS // 2
    product = frequency[:, None] * delays[None, :] % SAMPLES
    angle = product.astype(jnp.float32) * (2.0 * math.pi / SAMPLES)
    cosine = jnp.cos(angle)
    sine = jnp.sin(angle)
    upper = jnp.concatenate([cosine, sine], axis=1)
    lower = jnp.concatenate([-sine, cosine], axis=1)
    return (jnp.concatenate([upper, lower], axis=0) * (1.0 / math.sqrt(F))).astype(jnp.bfloat16)


def whiten(traces):
    signs = jnp.sign(traces)
    flat = signs.reshape(-1, SAMPLES)
    spectra = jnp.dot(
        flat, transform_table(), precision=lax.Precision.HIGHEST, preferred_element_type=jnp.float32
    )
    real_part = spectra[:, :F]
    imag_part = spectra[:, F:]
    power = real_part * real_part + imag_part * imag_part
    bands = jnp.mean(power.reshape(-1, F // WBLK, WBLK), axis=2)
    factor = 1.0 / jnp.sqrt(bands + 1e-05)
    factor = jnp.repeat(factor, WBLK, axis=1)
    white = jnp.concatenate([real_part * factor, imag_part * factor], axis=1).astype(jnp.bfloat16)
    return white.reshape(traces.shape[0], traces.shape[1], 2 * F)


def pair_terms(own_spectra, own_flags, far_spectra, far_flags, table):
    bin_count = own_spectra.shape[-1] // 2
    own_real = own_spectra[..., :bin_count].astype(jnp.float32)[:, None]
    own_imag = own_spectra[..., bin_count:].astype(jnp.float32)[:, None]
    far_real = far_spectra[..., :bin_count].astype(jnp.float32)[None]
    far_imag = far_spectra[..., bin_count:].astype(jnp.float32)[None]
    cross_real = own_real * far_real + own_imag * far_imag
    cross_imag = own_imag * far_real - own_real * far_imag
    cross = jnp.concatenate([cross_real, cross_imag], axis=-1).astype(jnp.bfloat16)
    lead = cross.shape[:3]
    analytic = jnp.dot(cross.reshape(-1, 2 * bin_count), table, preferred_element_type=jnp.float32)
    lag_count = table.shape[1] // 2
    analytic = analytic.reshape(lead + (2 * lag_count,))
    real_part = analytic[..., :lag_count]
    imag_part = analytic[..., lag_count:]
    magnitude = jnp.sqrt(real_part * real_part + imag_part * imag_part)
    divisor = jnp.maximum(magnitude, 0.5)
    weights = own_flags[:, None, :] * far_flags[None, :, :]
    linear = jnp.sum(weights[..., None] * real_part, axis=2)
    phase_real = jnp.sum(weights[..., None] * (real_part / divisor), axis=2)
    phase_imag = jnp.sum(weights[..., None] * (imag_part / divisor), axis=2)
    counts = jnp.sum(weights, axis=2)
    return (linear, phase_real, phase_imag, counts)


def local(traces, gap_mask, pair_mask):
    spectra = whiten(traces)
    gap_flags = gap_mask.astype(jnp.bfloat16)
    table = inverse_table()
    partners = [None] * (2 * REACH + 1)
    partners[REACH] = (spectra, gap_flags)
    upward = (spectra, gap_flags)
    downward = (spectra, gap_flags)
    for offset in range(1, REACH + 1):
        upward = passed_along((upward[0], upward[1]), "sta", -1)
        partners[REACH + offset] = upward
        downward = passed_along((downward[0], downward[1]), "sta", 1)
        partners[REACH - offset] = downward
    own_flags = gap_flags.astype(jnp.float32)
    results = [
        pair_terms(spectra, own_flags, partner[0], partner[1].astype(jnp.float32), table)
        for partner in partners
    ]
    linear = jnp.stack([item[0] for item in results], axis=1)
    phase_real = jnp.stack([item[1] for item in results], axis=1)
    phase_imag = jnp.stack([item[2] for item in results], axis=1)
    counts = jnp.stack([item[3] for item in results], axis=1)
    counts = lax.psum(counts, "win")
    linear, phase_real, phase_imag = (
        lax.psum_scatter(linear, "win", scatter_dimension=3, tiled=True),
        lax.psum_scatter(phase_real, "win", scatter_dimension=3, tiled=True),
        lax.psum_scatter(phase_imag, "win", scatter_dimension=3, tiled=True),
    )
    divisor = jnp.maximum(counts, 1.0)[..., None]
    phase_real = phase_real / divisor
    phase_imag = phase_imag / divisor
    return (
        linear
        / divisor
        * (phase_real * phase_real + phase_imag * phase_imag)
        * pair_mask.astype(jnp.float32)[..., None]
    )


def solution(mesh):
    return jax.shard_map(
        local,
        mesh=mesh,
        in_specs=(P("sta", "win", None), P("sta", "win"), P("sta", None, None)),
        out_specs=P("sta", None, None, "win"),
        check_vma=False,
    )
```

profile of v0, /device:TPU:0, one launch (start us, length us, event | category | flops | bytes accessed | tf_op | source)
XLA Modules:
  0.0 225.3 jit_solution(17679981926364892379)
XLA Ops:
  6.5 34.2 %sine_negate_fusion = (f32[2048,1024]{1,0:T(8,128)S(1)}, f32[2048,1024]{1,0:T(8,128)}) fusion(), kind=kLoop, calls=%fused_computation.12 | loop fusion | flops 31457280 | bytes 16777216 | tf_op jit(solution)/shard_map/neg | solution.py:26
  40.8 0.2 sign.3
  41.0 12.7 %fusion.33 = f32[128,2048]{1,0:T(8,128)S(1)} fusion(f32[128,2048]{1,0:T(8,128)S(1)} %bitcast.66, f32[2048,1024]{1,0:T(8,128)S(1)} %get-tuple-element.61, f32[2048,1024]{1,0:T(8,128)} %get-tuple-element.62), kind=kOutput, calls=%fused_computation.51 | convolution fusion | flops 6446645248 | bytes 18874368 | tf_op jit(solution)/shard_map/dot_general | solution.py:44
  53.8 0.0 copy-start.7
  53.8 0.1 add_bitcast_fusion
  53.9 0.1 copy.14
  54.0 0.2 reduce_sum.189
  54.3 0.1 copy.10
  54.4 0.2 broadcast_in_dim.2
  54.6 0.2 fusion.45
  54.8 3.4 %collective-permute-start.5 = (bf16[8,16,2048]{2,1,0:T(8,128)(2,1)S(1)}, bf16[8,16,2048]{2,1,0:T(8,128)(2,1)S(1)}, u32[]{:S(2)}, u32[]{:S(2)}) collective-permute-start(bf16[8,16,2048]{2,1,0:T(8,128)(2,1)S(1)} %pad_maximum_fusion), channel_id=1, source_target_pairs={{4,0},{8,4},{12,8},{16,12},{20,16},{24,20},{28,24},{0,28},{5,1},{9... | collective-permute-start | bytes 1572872 | tf_op jit(solution)/shard_map/ppermute | solution.py:18
  58.2 0.0 collective-permute-start.2
  58.2 2.6 %collective-permute-start.4 = (bf16[8,16]{1,0:T(8,128)(2,1)S(1)}, bf16[8,16]{1,0:T(8,128)(2,1)S(1)}, u32[]{:S(2)}, u32[]{:S(2)}) collective-permute-start(bf16[8,16]{1,0:T(8,128)(2,1)S(1)} %get-tuple-element.26), channel_id=1, source_target_pairs={{4,0},{8,4},{12,8},{16,12},{20,16},{24,20},{28,24},{0,28},{5,1},{9... | collective-permute-start | bytes 776 | tf_op jit(solution)/shard_map/ppermute | solution.py:18
  60.9 0.0 collective-permute-start
  60.9 8.8 %fusion.42 = (f32[1024,512]{1,0:T(8,128)S(1)}, f32[1024,512]{1,0:T(8,128)S(1)}, f32[1024,512]{1,0:T(8,128)S(1)}) fusion(s32[512]{0:T(512)S(1)} %iota_add_fusion), kind=kLoop, calls=%fused_computation.78 | loop fusion | flops 7864320 | bytes 6293504 | tf_op jit(solution)/shard_map/sin | solution.py:35
  69.7 0.0 collective-permute-done.4
  69.7 2.7 %collective-permute-start.6 = (bf16[8,16]{1,0:T(8,128)(2,1)S(1)}, bf16[8,16]{1,0:T(8,128)(2,1)S(1)}, u32[]{:S(2)}, u32[]{:S(2)}) collective-permute-start(bf16[8,16]{1,0:T(8,128)(2,1)S(1)} %collective-permute-done.4), channel_id=1, source_target_pairs={{4,0},{8,4},{12,8},{16,12},{20,16},{24,20},{28,24},{0,28},{5,1},{9... | collective-permute-start | bytes 776 | tf_op jit(solution)/shard_map/ppermute | solution.py:18
  72.5 0.0 collective-permute-done
  72.5 0.0 collective-permute-start.1
  72.6 1.2 collective-permute-done.6
  73.8 2.6 %collective-permute-done.1 = bf16[8,16]{1,0:T(8,128)(2,1)S(1)} collective-permute-done((bf16[8,16]{1,0:T(8,128)(2,1)S(1)}, bf16[8,16]{1,0:T(8,128)(2,1)S(1)}, u32[]{:S(2)}, u32[]{:S(2)}) %collective-permute-start.1) | collective-permute-done | bytes 288 | tf_op jit(solution)/shard_map/ppermute | solution.py:18
  76.4 0.0 collective-permute-done.5
  76.4 0.1 collective-permute-start.7
  76.5 0.7 fusion.51
  77.1 0.0 collective-permute-done.2
  77.1 0.4 collective-permute-start.3
  77.6 0.1 slice_convert_fusion.3
  77.7 0.1 slice_convert_fusion.5
  77.8 10.6 %collective-permute-done.7 = bf16[8,16,2048]{2,1,0:T(8,128)(2,1)S(1)} collective-permute-done((bf16[8,16,2048]{2,1,0:T(8,128)(2,1)S(1)}, bf16[8,16,2048]{2,1,0:T(8,128)(2,1)S(1)}, u32[]{:S(2)}, u32[]{:S(2)}) %collective-permute-start.7) | collective-permute-done | bytes 524320 | tf_op jit(solution)/shard_map/ppermute | solution.py:18
  88.4 0.1 slice_convert_fusion.1
  88.5 0.3 collective-permute-done.3
  88.8 0.1 slice_convert_fusion.7
  88.9 8.1 %add_convert_fusion = (bf16[8,8,16,1024]{3,2,1,0:T(8,128)(2,1)S(1)}, bf16[8,8,16,1024]{3,2,1,0:T(8,128)(2,1)S(1)}, bf16[8,8,16,1024]{3,2,1,0:T(8,128)(2,1)}, bf1...) fusion(f32[8,16,1024]{2,1,0:T(8,128)S(1)} %get-tuple-element.46, ...), kind=kLoop, calls=%fused_computation.38 | loop fusion | flops 41943040 | bytes 26214400 | tf_op jit(solution)/shard_map/convert
  97.0 6.8 %fusion.12 = f32[8,8,16,1024]{3,2,1,0:T(8,128)S(1)} fusion(bf16[8,8,16,1024]{3,2,1,0:T(8,128)(2,1)} %get-tuple-element.43, bf16[8,8,16,1024]{3,2,1,0:T(8,128)(2,1)} %get-tuple-element.44, f32[1024,512]{1,0:T(8,128)S(1)} %get-tuple-element.60, f32[1024,512]{1,0:T(8,128)S(1)} %get-tuple-element.59, f32[1024,512]{1,0:T(8,128)S(1)} %get-tuple-element.58), kind=kOutput, calls=%fused_computation.17 | convolution fusion | flops 4313841664 | bytes 14680064 | tf_op jit(solution)/shard_map/dot_general | solution.py:67
  103.8 2.2 multiply_reduce_fusion.14
  106.1 0.7 bitcast_dynamic-update-slice_fusion.14
  106.7 6.8 %fusion.16 = f32[8,8,16,1024]{3,2,1,0:T(8,128)S(1)} fusion(bf16[8,8,16,1024]{3,2,1,0:T(8,128)(2,1)} %get-tuple-element.37, bf16[8,8,16,1024]{3,2,1,0:T(8,128)(2,1)} %get-tuple-element.38, f32[1024,512]{1,0:T(8,128)S(1)} %get-tuple-element.60, f32[1024,512]{1,0:T(8,128)S(1)} %get-tuple-element.59, f32[1024,512]{1,0:T(8,128)S(1)} %get-tuple-element.58), kind=kOutput, calls=%fused_computation.21 | convolution fusion | flops 4313841664 | bytes 14680064 | tf_op jit(solution)/shard_map/dot_general | solution.py:67
  113.5 3.6 %multiply_reduce_fusion.13 = (f32[8,8,512]{2,1,0:T(8,128)S(1)}, f32[8,8,512]{2,1,0:T(8,128)S(1)}, f32[8,8,512]{2,1,0:T(8,128)}) fusion(f32[8,8,16,1024]{3,2,1,0:T(8,128)S(1)} %fusion.16, f32[8,8,16]{2,1,0:T(8,128)} %get-tuple-element.53), kind=kLoop, calls=%fused_computation.73 | loop fusion | flops 6193152 | bytes 4591616 | tf_op jit(solution)/shard_map/reduce_sum | solution.py:75
  117.1 0.7 bitcast_dynamic-update-slice_fusion.13
  117.8 7.0 %fusion.20 = f32[8,8,16,1024]{3,2,1,0:T(8,128)S(1)} fusion(bf16[8,8,16,1024]{3,2,1,0:T(8,128)(2,1)} %get-tuple-element.41, bf16[8,8,16,1024]{3,2,1,0:T(8,128)(2,1)} %get-tuple-element.42, f32[1024,512]{1,0:T(8,128)S(1)} %get-tuple-element.60, f32[1024,512]{1,0:T(8,128)S(1)} %get-tuple-element.59, f32[1024,512]{1,0:T(8,128)S(1)} %get-tuple-element.58), kind=kOutput, calls=%fused_computation.25 | convolution fusion | flops 4313841664 | bytes 14680064 | tf_op jit(solution)/shard_map/dot_general | solution.py:67
  124.8 3.6 %multiply_reduce_fusion.12 = (f32[8,8,512]{2,1,0:T(8,128)S(1)}, f32[8,8,512]{2,1,0:T(8,128)S(1)}, f32[8,8,512]{2,1,0:T(8,128)}) fusion(f32[8,8,16,1024]{3,2,1,0:T(8,128)S(1)} %fusion.20, f32[8,8,16]{2,1,0:T(8,128)} %get-tuple-element.57), kind=kLoop, calls=%fused_computation.72 | loop fusion | flops 6193152 | bytes 4591616 | tf_op jit(solution)/shard_map/reduce_sum | solution.py:75
  128.4 0.7 bitcast_dynamic-update-slice_fusion.12
  129.1 4.5 %fusion.24 = f32[8,8,16,1024]{3,2,1,0:T(8,128)S(1)} fusion(bf16[8,8,16,1024]{3,2,1,0:T(8,128)(2,1)S(1)} %get-tuple-element.39, bf16[8,8,16,1024]{3,2,1,0:T(8,128)(2,1)S(1)} %get-tuple-element.40, f32[1024,512]{1,0:T(8,128)S(1)} %get-tuple-element.60, f32[1024,512]{1,0:T(8,128)S(1)} %get-tuple-element.59, f32[1024,512]{1,0:T(8,128)S(1)} %get-tuple-element.58), kind=kOutput, calls=%fused_computation.29 | convolution fusion | flops 4313841664 | bytes 14680064 | tf_op jit(solution)/shard_map/dot_general | solution.py:67
  133.6 2.9 %multiply_reduce_fusion.11 = (f32[8,8,512]{2,1,0:T(8,128)S(1)}, f32[8,8,512]{2,1,0:T(8,128)S(1)}, f32[8,8,512]{2,1,0:T(8,128)S(1)}) fusion(f32[8,8,16,1024]{3,2,1,0:T(8,128)S(1)} %fusion.24, f32[8,8,16]{2,1,0:T(8,128)} %get-tuple-element.54), kind=kLoop, calls=%fused_computation.71 | loop fusion | flops 6193152 | bytes 4591616 | tf_op jit(solution)/shard_map/reduce_sum | solution.py:75
  136.6 0.7 bitcast_dynamic-update-slice_fusion.11
  137.3 4.8 %fusion.28 = f32[8,8,16,1024]{3,2,1,0:T(8,128)S(1)} fusion(bf16[8,8,16,1024]{3,2,1,0:T(8,128)(2,1)S(1)} %get-tuple-element.28, bf16[8,8,16,1024]{3,2,1,0:T(8,128)(2,1)S(1)} %get-tuple-element.27, f32[1024,512]{1,0:T(8,128)S(1)} %get-tuple-element.60, f32[1024,512]{1,0:T(8,128)S(1)} %get-tuple-element.59, f32[1024,512]{1,0:T(8,128)S(1)} %get-tuple-element.58), kind=kOutput, calls=%fused_computation.33 | convolution fusion | flops 4313841664 | bytes 14680064 | tf_op jit(solution)/shard_map/dot_general | solution.py:67
  142.1 0.0 copy-start.3
  142.1 0.0 copy-start.6
  142.1 2.2 multiply_reduce_fusion.10
  144.3 0.7 bitcast_dynamic-update-slice_fusion.10
  145.0 0.0 reduce-scatter.4.cloned.1.call-update
  145.0 0.0 reduce-scatter.6.cloned.1.call-start
  145.1 0.0 copy-done.4
  145.1 0.0 copy-start.2
  145.2 0.8 copy-done.2
  146.0 0.0 reduce-scatter.6.cloned.1.call-update
  146.0 0.0 reduce-scatter.8.cloned.1.call-start
  146.2 0.8 copy-done.1
  147.0 0.0 reduce-scatter.8.cloned.1.call-update
  147.1 19.7 %psum.7 = f32[8,5,8]{2,0,1:T(8,128)S(1)} all-reduce(f32[8,5,8]{2,0,1:T(8,128)S(1)} %constant_dynamic-update-slice_fusion), channel_id=1, replica_groups=mesh['sta'=8,'win'=4] {'win'}, use_global_device_ids=true, to_apply=%region_12.13 | all-reduce | flops 320 | bytes 2560 | tf_op jit(solution)/shard_map/psum | solution.py:104
  166.9 3.0 %reduce-scatter.4.cloned.1.call-done = f32[8,5,8,128]{3,2,1,0:T(8,128)} async-done(((f32[8,5,8,512]{3,2,1,0:T(8,128)}), f32[8,5,8,128]{3,2,1,0:T(8,128)}) %reduce-scatter.4.cloned.1.call-update) | async-done | bytes 163856 | tf_op jit(solution)/shard_map/reduce_scatter | solution.py:106
  169.9 23.4 %reduce-scatter.6.cloned.1.call-done = f32[8,5,8,128]{3,2,1,0:T(8,128)} async-done(((f32[8,5,8,512]{3,2,1,0:T(8,128)}), f32[8,5,8,128]{3,2,1,0:T(8,128)}) %reduce-scatter.6.cloned.1.call-update) | async-done | bytes 163856 | tf_op jit(solution)/shard_map/reduce_scatter | solution.py:107
  193.3 23.4 %reduce-scatter.8.cloned.1.call-done = f32[8,5,8,128]{3,2,1,0:T(8,128)} async-done(((f32[8,5,8,512]{3,2,1,0:T(8,128)}), f32[8,5,8,128]{3,2,1,0:T(8,128)}) %reduce-scatter.8.cloned.1.call-update) | async-done | bytes 163856 | tf_op jit(solution)/shard_map/reduce_scatter | solution.py:108
  216.6 1.9 multiply_multiply_fusion
  (40 shorter events, 0.4 us)
Async XLA Ops:
  6.5 34.2 %copy-start = (f32[8,16,2048]{2,1,0:T(8,128)S(1)}, f32[8,16,2048]{2,1,0:T(8,128)}, u32[]{:S(2)}) copy-start(f32[8,16,2048]{2,1,0:T(8,128)} %param.3) | copy-start | bytes 3145732
  6.5 163.3 %reduce-scatter.4.cloned.1.call-start = ((), (), s32[]{:S(2)}) async-start(), calls=%async_computation.3 | async-start | bytes 819200 | tf_op jit(solution)/shard_map/reduce_scatter | solution.py:106
  53.8 4.4 %copy-start.7 = (s32[8,16]{1,0:T(8,128)S(1)}, s32[8,16]{1,0:T(8,128)}, u32[]{:S(2)}) copy-start(s32[8,16]{1,0:T(8,128)} %param.4) | copy-start | bytes 1540
  54.8 21.6 %collective-permute-start.5 = (bf16[8,16,2048]{2,1,0:T(8,128)(2,1)S(1)}, bf16[8,16,2048]{2,1,0:T(8,128)(2,1)S(1)}, u32[]{:S(2)}, u32[]{:S(2)}) collective-permute-start(bf16[8,16,2048]{2,1,0:T(8,128)(2,1)S(1)} %pad_maximum_fusion), channel_id=1, source_target_pairs={{4,0},{8,4},{12,8},{16,12},{20,16},{24,20},{28,24},{0,28},{5,1},{9... | collective-permute-start | bytes 1572872 | tf_op jit(solution)/shard_map/ppermute | solution.py:18
  58.2 18.9 %collective-permute-start.2 = (bf16[8,16,2048]{2,1,0:T(8,128)(2,1)S(1)}, bf16[8,16,2048]{2,1,0:T(8,128)(2,1)S(1)}, u32[]{:S(2)}, u32[]{:S(2)}) collective-permute-start(bf16[8,16,2048]{2,1,0:T(8,128)(2,1)S(1)} %pad_maximum_fusion), channel_id=1, source_target_pairs={{28,0},{0,4},{4,8},{8,12},{12,16},{16,20},{20,24},{24,28},{29,1},{... | collective-permute-start | bytes 1572872 | tf_op jit(solution)/shard_map/ppermute | solution.py:18
  58.2 11.5 %collective-permute-start.4 = (bf16[8,16]{1,0:T(8,128)(2,1)S(1)}, bf16[8,16]{1,0:T(8,128)(2,1)S(1)}, u32[]{:S(2)}, u32[]{:S(2)}) collective-permute-start(bf16[8,16]{1,0:T(8,128)(2,1)S(1)} %get-tuple-element.26), channel_id=1, source_target_pairs={{4,0},{8,4},{12,8},{16,12},{20,16},{24,20},{28,24},{0,28},{5,1},{9... | collective-permute-start | bytes 776 | tf_op jit(solution)/shard_map/ppermute | solution.py:18
  60.9 11.6 %collective-permute-start = (bf16[8,16]{1,0:T(8,128)(2,1)S(1)}, bf16[8,16]{1,0:T(8,128)(2,1)S(1)}, u32[]{:S(2)}, u32[]{:S(2)}) collective-permute-start(bf16[8,16]{1,0:T(8,128)(2,1)S(1)} %get-tuple-element.26), channel_id=1, source_target_pairs={{28,0},{0,4},{4,8},{8,12},{12,16},{16,20},{20,24},{24,28},{29,1},{... | collective-permute-start | bytes 776 | tf_op jit(solution)/shard_map/ppermute | solution.py:18
  69.7 4.0 %collective-permute-start.6 = (bf16[8,16]{1,0:T(8,128)(2,1)S(1)}, bf16[8,16]{1,0:T(8,128)(2,1)S(1)}, u32[]{:S(2)}, u32[]{:S(2)}) collective-permute-start(bf16[8,16]{1,0:T(8,128)(2,1)S(1)} %collective-permute-done.4), channel_id=1, source_target_pairs={{4,0},{8,4},{12,8},{16,12},{20,16},{24,20},{28,24},{0,28},{5,1},{9... | collective-permute-start | bytes 776 | tf_op jit(solution)/shard_map/ppermute | solution.py:18
  72.5 3.9 %collective-permute-start.1 = (bf16[8,16]{1,0:T(8,128)(2,1)S(1)}, bf16[8,16]{1,0:T(8,128)(2,1)S(1)}, u32[]{:S(2)}, u32[]{:S(2)}) collective-permute-start(bf16[8,16]{1,0:T(8,128)(2,1)S(1)} %collective-permute-done), channel_id=1, source_target_pairs={{28,0},{0,4},{4,8},{8,12},{12,16},{16,20},{20,24},{24,28},{29,1},{... | collective-permute-start | bytes 776 | tf_op jit(solution)/shard_map/ppermute | solution.py:18
  76.4 12.0 %collective-permute-start.7 = (bf16[8,16,2048]{2,1,0:T(8,128)(2,1)S(1)}, bf16[8,16,2048]{2,1,0:T(8,128)(2,1)S(1)}, u32[]{:S(2)}, u32[]{:S(2)}) collective-permute-start(bf16[8,16,2048]{2,1,0:T(8,128)(2,1)S(1)} %collective-permute-done.5), channel_id=1, source_target_pairs={{4,0},{8,4},{12,8},{16,12},{20,16},{24,20},{28,24},{0,28},{5,1},{9... | collective-permute-start | bytes 1572872 | tf_op jit(solution)/shard_map/ppermute | solution.py:18
  77.1 11.7 %collective-permute-start.3 = (bf16[8,16,2048]{2,1,0:T(8,128)(2,1)S(1)}, bf16[8,16,2048]{2,1,0:T(8,128)(2,1)S(1)}, u32[]{:S(2)}, u32[]{:S(2)}) collective-permute-start(bf16[8,16,2048]{2,1,0:T(8,128)(2,1)S(1)} %collective-permute-done.2), channel_id=1, source_target_pairs={{28,0},{0,4},{4,8},{8,12},{12,16},{16,20},{20,24},{24,28},{29,1},{... | collective-permute-start | bytes 1572872 | tf_op jit(solution)/shard_map/ppermute | solution.py:18
  137.3 4.8 %copy-start.5 = (f32[8,8,16]{2,1,0:T(8,128)S(1)}, f32[8,8,16]{2,1,0:T(8,128)}, u32[]{:S(2)}) copy-start(f32[8,8,16]{2,1,0:T(8,128)} %get-tuple-element.56) | copy-start | bytes 12292
  142.1 3.0 %copy-start.3 = (f32[8,8,512]{2,1,0:T(8,128)S(1)}, f32[8,8,512]{2,1,0:T(8,128)}, u32[]{:S(2)}) copy-start(f32[8,8,512]{2,1,0:T(8,128)} %get-tuple-element.16) | copy-start | bytes 393220
  142.1 3.0 %copy-start.4 = (f32[8,8,512]{2,1,0:T(8,128)S(1)}, f32[8,8,512]{2,1,0:T(8,128)}, u32[]{:S(2)}) copy-start(f32[8,8,512]{2,1,0:T(8,128)} %get-tuple-element.13) | copy-start | bytes 393220
  142.1 4.0 %copy-start.6 = (s32[8,5,8]{2,0,1:T(8,128)S(1)}, s32[8,5,8]{2,0,1:T(8,128)}, u32[]{:S(2)}) copy-start(s32[8,5,8]{2,0,1:T(8,128)} %param.5) | copy-start | bytes 3844
  145.0 48.3 %reduce-scatter.6.cloned.1.call-start = ((), (), s32[]{:S(2)}) async-start(), calls=%async_computation.4 | async-start | bytes 819200 | tf_op jit(solution)/shard_map/reduce_scatter | solution.py:107
  145.1 0.8 copy-start.2
  146.0 70.6 %reduce-scatter.8.cloned.1.call-start = ((), (), s32[]{:S(2)}) async-start(), calls=%async_computation.5 | async-start | bytes 819200 | tf_op jit(solution)/shard_map/reduce_scatter | solution.py:108
  146.2 0.9 copy-start.1
Sparse Core Ops, SparseCore 0:
  145.1 24.7 reduce-scatter.3
  172.2 21.0 reduce-scatter.5
  195.6 21.0 reduce-scatter.7
where the time goes:
time: 228 us; the launch traced here: 225 us
  other arithmetic  69.6 us (31%)
  waiting for transfers between devices  64.5 us (28%)
  matrix products  42.6 us (19%)
  blocking collectives  19.7 us (9%)
  between operations  13.8 us (6%)
  starting transfers between devices  9.37 us (4%)
  local copies, waits for them, and re-layouts  5.72 us (3%)
    neg x1, other arithmetic, transform_table(): return jnp.concatenate([jnp.cos(angle), -jnp.sin(angle)], axis=1)  34.2 us
    dot_general x5, matrix products, pair_terms(): jnp.dot(cross.reshape(-1, 2 * bin_count), table, preferred_element_type=j...  29.8 us
    reduce_scatter x1, waiting for transfers between devices, local(): lax.psum_scatter(phase_real, 'win', scatter_dimension=3, tiled=True)  23.4 us
    reduce_scatter x1, waiting for transfers between devices, local(): lax.psum_scatter(phase_imag, 'win', scatter_dimension=3, tiled=True)  23.4 us
    psum x1, blocking collectives, local(): counts = lax.psum(counts, 'win')  19.7 us
    ppermute x8, waiting for transfers between devices, passed_along(): return lax.ppermute(block, axis, route)  14.7 us
    reduce_sum x5, other arithmetic, pair_terms(): linear = jnp.sum(weights[..., None] * real_part, axis=2)  14.6 us
    dot_general x1, matrix products, whiten(): jnp.dot(flat, transform_table(), precision=lax.Precision.HIGHEST, preferr...  12.7 us
  transfers between devices with their start and end apart: 11, of which 7 were waited for; matrix products, arithmetic and copies ran while one was open for 4% of the time, Pallas kernels for 0%

commit v1 on v0

v1 whole, which is shorter than its diff:
```python
import functools
import math

import jax
import jax.numpy as jnp
import ml_dtypes
import numpy as np
from jax import lax
from jax.experimental import pallas as pl
from jax.experimental.pallas import tpu as pltpu
from jax.sharding import PartitionSpec as P

SAMPLES = 2048
F = 1024
LAGS = 512
WBLK = 128
REACH = 2
LANES = 128
SLICES = F // LANES
HALF = LAGS // 2
PEAK = 34.0
EXTRA = 16
STACK = 4


def bins():
    m = np.arange(LANES // 2)
    rows = [np.concatenate([16 * m, 8 + 16 * m])]
    for s in range(1, SLICES):
        rows.append(np.concatenate([s + 16 * m, 16 - s + 16 * m]))
    return np.stack(rows)


def split(table):
    high = table.astype(ml_dtypes.bfloat16)
    low = (table - high.astype(np.float64)).astype(ml_dtypes.bfloat16)
    return high, low


def forward_tables():
    at = bins()
    t = np.arange(LANES)
    upper = (np.arange(LANES) >= LANES // 2)[None, :]
    tables = []
    for s in range(SLICES):
        angle = 2.0 * np.pi * ((t[:, None] * at[s][None, :]) % SAMPLES) / SAMPLES
        c, n = np.cos(angle), np.sin(angle)
        if s == 0:
            first = np.concatenate([np.where(upper, 0.0, c), np.where(upper, 0.0, -n)], axis=1)
            second = np.concatenate([np.where(upper, c, 0.0), np.where(upper, -n, 0.0)], axis=1)
        else:
            first = np.concatenate([c, -n], axis=1)
            second = np.concatenate([np.where(upper, -n, n), np.where(upper, -c, c)], axis=1)
        tables.append(np.concatenate([first, second], axis=0))
    return split(np.stack(tables))


def band_table():
    band = (np.arange(LANES) % (LANES // 2)) // (WBLK // 16)
    return (band[:, None] == band[None, :]).astype(np.float32)


def inverse_table():
    at = bins().reshape(-1)
    tau = np.arange(HALF)
    angle = (((at[:, None] * tau[None, :]) % SAMPLES).astype(np.float32)) * np.float32(2.0 * math.pi / SAMPLES)
    both = np.concatenate([np.cos(angle), np.sin(angle)], axis=1).astype(np.float32)
    return (both * np.float32(1.0 / math.sqrt(F))).astype(ml_dtypes.bfloat16)


def edge_table():
    scale = 1.0 / math.sqrt(F)
    sign = np.where(np.arange(LANES) < LANES // 2, 1.0, -1.0) * scale
    table = np.zeros((4 * LANES, 2 * LANES))
    cr, sr, ci, si = (slice(k * LANES, (k + 1) * LANES) for k in range(4))
    table[cr, 0], table[si, 0] = scale, -sign
    table[cr, 1], table[si, 1] = scale, sign
    table[sr, LANES], table[ci, LANES] = sign, scale
    table[sr, LANES + 1], table[ci, LANES + 1] = -sign, scale
    return table.astype(ml_dtypes.bfloat16)


ROOT = float(np.float32(ml_dtypes.bfloat16(math.sqrt(0.5))))


def stage_one(x):
    r = math.sqrt(0.5)
    a = [x[s] + x[s + 8] for s in range(8)]
    b = [x[s] - x[s + 8] for s in range(8)]
    c = [a[s] + a[s + 4] for s in range(4)]
    d = [a[s] - a[s + 4] for s in range(4)]
    e0, e1, g0, g1 = c[0] + c[2], c[1] + c[3], c[0] - c[2], c[1] - c[3]
    pairs = [None] * 8
    pairs[0] = (e0 + e1, e0 - e1)
    pairs[4] = (g0, -g1)
    near, far = r * (d[1] - d[3]), r * (d[1] + d[3])
    pairs[2] = (d[0] + near, -(d[2] + far))
    pairs[6] = (d[0] - near, d[2] - far)
    u = [None] + [b[s] - b[8 - s] for s in (1, 2, 3)]
    v = [None] + [b[s] + b[8 - s] for s in (1, 2, 3)]
    for k in (1, 3, 5, 7):
        real = b[0]
        imag = b[4] * math.sin(math.pi * k / 2)
        for s in (1, 2, 3):
            real = real + u[s] * math.cos(math.pi * s * k / 8)
            imag = imag + v[s] * math.sin(math.pi * s * k / 8)
        pairs[k] = (real, -imag)
    return pairs


def forward_kernel(stations, windows, traces, gaps, high, low, band, out, first, second):
    rows = stations * windows
    block = 16
    for start in range(0, rows, block):
        x = traces[start:start + block, :]
        x = jnp.where(x > 0, 1.0, jnp.where(x < 0, -1.0, 0.0))
        y = stage_one([x[:, s * LANES:(s + 1) * LANES] for s in range(16)])
        for s in range(SLICES):
            both = jnp.concatenate(y[s], axis=1)
            top = both.astype(jnp.bfloat16)
            first[s, start:start + block, :] = top
            second[s, start:start + block, :] = (both - top.astype(jnp.float32)).astype(jnp.bfloat16)
    spectra = []
    power = jnp.zeros((rows, LANES), jnp.float32)
    for s in range(SLICES):
        z = jnp.dot(first[s], high[s], preferred_element_type=jnp.float32)
        z += jnp.dot(second[s], high[s], preferred_element_type=jnp.float32)
        z += jnp.dot(first[s], low[s], preferred_element_type=jnp.float32)
        spectra.append(z)
        power += z[:, :LANES] * z[:, :LANES] + z[:, LANES:] * z[:, LANES:]
    bands = jnp.dot(power, band[...], precision=lax.Precision.HIGHEST, preferred_element_type=jnp.float32)
    factor = lax.rsqrt(bands * (1.0 / WBLK) + 1e-05)
    flags = gaps[...].astype(jnp.float32)
    keep = jnp.concatenate(
        [jnp.broadcast_to(flags[:, w:w + 1], (stations, LANES)) for w in range(windows)], axis=0
    )
    corner = lax.broadcasted_iota(jnp.int32, (rows, LANES), 1) == 0
    to = lax.broadcasted_iota(jnp.int32, (rows, rows), 0)
    source = lax.broadcasted_iota(jnp.int32, (rows, rows), 1)
    moved = (to // stations == source % windows) & (to % stations == source // windows)
    moved = jnp.where(moved, 1.0, 0.0).astype(jnp.bfloat16)
    factor = jnp.concatenate([factor, factor], axis=1)
    keep = jnp.concatenate([keep, keep], axis=1)
    for s in range(SLICES):
        white = (spectra[s] * factor).astype(jnp.bfloat16)
        white = jnp.dot(moved, white, preferred_element_type=jnp.float32) * keep
        real, imag = white[:, :LANES], white[:, LANES:]
        if s == 0:
            imag = jnp.where(corner, keep[:, :LANES], imag)
        out[:, s * LANES:(s + 1) * LANES] = real.astype(jnp.bfloat16)
        out[:, F + s * LANES:F + (s + 1) * LANES] = imag.astype(jnp.bfloat16)


def forward(traces, gaps):
    stations, windows, samples = traces.shape
    rows = stations * windows
    high, low = forward_tables()
    return pl.pallas_call(
        functools.partial(forward_kernel, stations, windows),
        out_shape=jax.ShapeDtypeStruct((rows, 2 * F), jnp.bfloat16),
        scratch_shapes=[pltpu.VMEM((SLICES, rows, 2 * LANES), jnp.bfloat16)] * 2,
        compiler_params=pltpu.CompilerParams(vmem_limit_bytes=40 * 1024 * 1024),
        cost_estimate=pl.CostEstimate(flops=6 * rows * F * 512, bytes_accessed=4 << 20, transcendentals=rows * LANES),
        name="whiten",
    )(traces.reshape(rows, samples), gaps, jnp.asarray(high), jnp.asarray(low), jnp.asarray(band_table()))


def unit_kernel(stations, windows, parts, choose, *refs):
    x_ref, refs = refs[0], refs[1:]
    y_refs, refs = refs[:2 if choose else 1], refs[2 if choose else 1:]
    table, edge = refs[:2]
    outs = refs[2:2 + parts]
    xf, yf, x0, y0, cross, fold, total, edges, counts = refs[2 + parts:]
    pairs = stations * stations
    rows = stations * windows
    me = lax.axis_index("win")

    def load(source, target, corner):
        lane = lax.broadcasted_iota(jnp.int32, (rows, LANES), 1) == 0
        for s in range(2 * SLICES):
            at = slice(s * LANES, (s + 1) * LANES)
            value = source[:, at].astype(jnp.float32)
            if s == SLICES:
                corner[...] = value.reshape(corner.shape)
                value = jnp.where(lane, 0.0, value)
            target[:, :, at] = value.reshape(windows, stations, LANES)

    load(x_ref, xf, x0)
    if choose:
        odd = lax.rem(lax.axis_index("sta"), 2)

        @pl.when(odd == 0)
        def _():
            load(y_refs[0], yf, y0)

        @pl.when(odd == 1)
        def _():
            load(y_refs[1], yf, y0)
    else:
        load(y_refs[0], yf, y0)

    total[...] = jnp.zeros_like(total)
    edges[...] = jnp.zeros_like(edges)
    counts[...] = jnp.zeros_like(counts)

    def step(chunk, carry):
        for v in range(STACK):
            w = chunk * STACK + v
            for i in range(0, stations, 2):
                folded = [[], [], [], []]
                for e in range(2):
                    at = pl.ds((i + e) * stations, stations)
                    counts[at, :] += x0[w, i + e:i + e + 1, :] * y0[w]
                place = pl.ds(v * pairs + i * stations, 2 * stations)
                reals, imags = [], []
                for s in range(SLICES):
                    re = slice(s * LANES, (s + 1) * LANES)
                    im = slice(F + s * LANES, F + (s + 1) * LANES)
                    yr, yi = yf[w, :, re], yf[w, :, im]
                    halves = []
                    for e in range(2):
                        xr, xi = xf[w, i + e:i + e + 1, re], xf[w, i + e:i + e + 1, im]
                        halves.append((xr * yr + xi * yi, xi * yr - xr * yi))
                    cr = jnp.concatenate([h[0] for h in halves], axis=0)
                    ci = jnp.concatenate([h[1] for h in halves], axis=0)
                    reals.append(cr)
                    imags.append(ci)
                    cross[0, place, re] = cr.astype(jnp.bfloat16)
                    cross[1, place, re] = ci.astype(jnp.bfloat16)
                for k, c in enumerate((reals, imags)):
                    cosine = (c[0] - c[4]) + ROOT * ((c[1] + c[7]) - (c[3] + c[5]))
                    sine = (c[2] - c[6]) + ROOT * ((c[1] + c[3]) - (c[5] + c[7]))
                    fold[place, 2 * k * LANES:(2 * k + 1) * LANES] = cosine.astype(jnp.bfloat16)
                    fold[place, (2 * k + 1) * LANES:(2 * k + 2) * LANES] = sine.astype(jnp.bfloat16)
        from_real = jnp.dot(cross[0], table[...], preferred_element_type=jnp.float32)
        from_imag = jnp.dot(cross[1], table[...], preferred_element_type=jnp.float32)
        rim = jnp.dot(fold[...], edge[...], preferred_element_type=jnp.float32)
        sums = [None] * 9
        for v in range(STACK):
            at = slice(v * pairs, (v + 1) * pairs)
            p, r = from_real[at, :HALF], from_real[at, HALF:]
            s, q = from_imag[at, :HALF], from_imag[at, HALF:]
            terms = []
            for real, imag in ((p - q, r + s), (p + q, s - r), (rim[at, :LANES], rim[at, LANES:])):
                scale = lax.rsqrt(jnp.maximum(real * real + imag * imag, 0.25))
                terms += [real, real * scale, imag * scale]
            sums = terms if v == 0 else [a + b for a, b in zip(sums, terms)]
        for k in range(6):
            total[k] += sums[k]
        for k in range(3):
            edges[k] += sums[6 + k]
        return carry

    lax.fori_loop(0, windows // STACK, step, 0)

    scales = (32766.0 / (PEAK * windows), 32000.0 / windows, 32000.0 / windows)
    wide = LAGS // parts

    def piece(z):
        if z < parts // 2:
            return 1, (parts // 2 - 1 - z) * wide
        return 0, (z - parts // 2) * wide

    lane = lax.broadcasted_iota(jnp.int32, (pairs, LANES), 1)
    last = jnp.zeros((pairs, LANES), jnp.float32)
    for z in range(parts):
        side, start = piece(z)
        for k in range(3):
            if start + wide < HALF:
                column = total[3 * side + k, :, start + wide:start + wide + 1]
            else:
                column = edges[k, :, side:side + 1]
            last = jnp.where(lane == 4 * z + k, column * scales[k], last)
        last = jnp.where(lane == 4 * z + 3, counts[:, 0:1], last)
    turned = jnp.transpose(last)

    def whole(value):
        return jnp.round(value).astype(jnp.int32).astype(jnp.int16)

    for here in range(parts):
        @pl.when(me == here)
        def _():
            for d in range(parts):
                z = here ^ d
                side, start = piece(z)
                for k in range(3):
                    part = total[3 * side + k, :, start:start + wide] * scales[k]
                    outs[d][k * pairs:(k + 1) * pairs, 0:wide] = whole(part)
                tail = turned[4 * z:4 * z + 4]
                tail = jnp.concatenate([tail, jnp.zeros((EXTRA - 4, pairs), jnp.float32)], axis=0)
                outs[d][3 * pairs:3 * pairs + EXTRA, 0:pairs] = whole(tail)


def unit(stations, parts, own, others, name):
    rows = own.shape[0]
    windows = rows // stations
    pairs = stations * stations
    choose = len(others) == 2
    shape = jax.ShapeDtypeStruct((3 * pairs + EXTRA, LANES), jnp.int16)
    return pl.pallas_call(
        functools.partial(unit_kernel, stations, windows, parts, choose),
        out_shape=[shape] * parts,
        scratch_shapes=[
            pltpu.VMEM((windows, stations, 2 * F), jnp.float32),
            pltpu.VMEM((windows, stations, 2 * F), jnp.float32),
            pltpu.VMEM((windows, stations, LANES), jnp.float32),
            pltpu.VMEM((windows, stations, LANES), jnp.float32),
            pltpu.VMEM((2, STACK * pairs, F), jnp.bfloat16),
            pltpu.VMEM((STACK * pairs, 4 * LANES), jnp.bfloat16),
            pltpu.VMEM((6, pairs, HALF), jnp.float32),
            pltpu.VMEM((3, pairs, LANES), jnp.float32),
            pltpu.VMEM((pairs, LANES), jnp.float32),
        ],
        compiler_params=pltpu.CompilerParams(vmem_limit_bytes=48 * 1024 * 1024),
        cost_estimate=pl.CostEstimate(
            flops=4 * rows * stations * F * LAGS, bytes_accessed=3 << 20, transcendentals=rows * stations * LAGS
        ),
        name=name,
    )(own, *others, jnp.asarray(inverse_table()), jnp.asarray(edge_table()))


def finish_kernel(stations, windows, parts, back, *refs):
    sums = refs[:parts]
    outs = refs[parts:]
    pairs = stations * stations
    wide = LAGS // parts
    me = lax.axis_index("win")
    acc = sums[0][...].astype(jnp.int32).astype(jnp.float32)
    for ref in sums[1:]:
        acc = acc + ref[...].astype(jnp.int32).astype(jnp.float32)
    scales = (PEAK * windows / 32766.0, windows / 32000.0, windows / 32000.0)
    tail = jnp.transpose(acc[3 * pairs:])[:pairs]
    inverse = 1.0 / jnp.maximum(tail[:, 3:4], 1.0)

    def stack(linear, real, imag):
        linear = linear * scales[0] * inverse
        real = real * scales[1] * inverse
        imag = imag * scales[2] * inverse
        return linear * (real * real + imag * imag)

    plain = stack(acc[:pairs], acc[pairs:2 * pairs], acc[2 * pairs:3 * pairs])
    edge = stack(tail[:, 0:1], tail[:, 1:2], tail[:, 2:3])
    row = lax.broadcasted_iota(jnp.int32, (LANES, LANES), 0)
    column = lax.broadcasted_iota(jnp.int32, (LANES, LANES), 1)
    mirror = jnp.where((row + column == wide) & (column > 0) & (column < wide), 1.0, 0.0)
    turned = jnp.dot(plain, mirror, precision=lax.Precision.HIGHEST, preferred_element_type=jnp.float32)
    lane = lax.broadcasted_iota(jnp.int32, (pairs, LANES), 1)
    turned = jnp.where(lane == 0, edge, turned)
    negative = me < parts // 2
    outs[0][...] = jnp.where(negative, turned, plain)
    if back:
        value = jnp.where(negative, plain, turned)
        row = lax.broadcasted_iota(jnp.int32, (pairs, pairs), 0)
        column = lax.broadcasted_iota(jnp.int32, (pairs, pairs), 1)
        swap = (row // stations == column % stations) & (row % stations == column // stations)
        swap = jnp.where(swap, 1.0, 0.0)
        outs[1][...] = jnp.dot(swap, value, precision=lax.Precision.HIGHEST, preferred_element_type=jnp.float32)


def finish(stations, windows, sums, back, name):
    pairs = stations * stations
    parts = len(sums)
    shape = jax.ShapeDtypeStruct((pairs, LANES), jnp.float32)
    return pl.pallas_call(
        functools.partial(finish_kernel, stations, windows, parts, back),
        out_shape=[shape] * (2 if back else 1),
        compiler_params=pltpu.CompilerParams(vmem_limit_bytes=16 * 1024 * 1024),
        cost_estimate=pl.CostEstimate(flops=1 << 22, bytes_accessed=1 << 18, transcendentals=0),
        name=name,
    )(*sums)


def exchange(sums):
    parts = len(sums)
    return [sums[0]] + [
        lax.ppermute(sums[d], "win", [(i, i ^ d) for i in range(parts)]) for d in range(1, parts)
    ]


def local(traces, gap_mask, pair_mask):
    blocks = lax.axis_size("sta")
    parts = lax.axis_size("win")
    stations, windows, _ = traces.shape
    white = forward(traces, gap_mask)
    second = lax.ppermute(white, "sta", [((i + 2) % blocks, i) for i in range(blocks)])
    beside = lax.ppermute(white, "sta", [(i ^ 1, i) for i in range(blocks)])
    self_sums = exchange(unit(stations, parts, white, [white], "stack0"))
    handed = lax.ppermute(second, "sta", [(i ^ 1, i) for i in range(blocks)])
    far_sums = exchange(unit(stations, parts, white, [second], "stack2"))
    near_sums = exchange(unit(stations, parts, white, [beside, handed], "stack1"))

    def returned(value, distance):
        route = []
        for b in range(blocks):
            for z in range(parts):
                route.append((b * parts + z, ((b + distance) % blocks) * parts + parts - 1 - z))
        return lax.ppermute(value, ("sta", "win"), route)

    (middle,) = finish(stations, windows, self_sums, False, "finish0")
    far, far_back = finish(stations, windows, far_sums, True, "finish2")
    far_back = returned(far_back, 2)
    near, near_back = finish(stations, windows, near_sums, True, "finish1")
    near_back = returned(near_back, 1)
    wide = LAGS // parts
    pws = jnp.stack(
        [value.reshape(stations, stations, LANES)[..., :wide] for value in (far_back, near_back, middle, near, far)], axis=1
    )
    return pws * pair_mask.astype(jnp.float32)[..., None]


def solution(mesh):
    return jax.shard_map(
        local,
        mesh=mesh,
        in_specs=(P("sta", "win", None), P("sta", "win"), P("sta", None, None)),
        out_specs=P("sta", None, None, "win"),
        check_vma=False,
    )
```

time: 228 us -> 65.6 us (0.29); the launches traced: 225 us -> 65.3 us
  other arithmetic: 69.6 us -> 0.78 us
  waiting for transfers between devices: 64.5 us -> 18.1 us
  matrix products: 42.6 us -> 0 us
  blocking collectives: 19.7 us -> 0 us
  Pallas kernels: 0 us -> 18.1 us
  between operations: 13.8 us -> 0.14 us
  starting transfers between devices: 9.37 us -> 22.8 us
    reduce_scatter x3 -> x0, waiting for transfers between devices: 49.7 us -> none  [the longest x1 23.4 us: local(): lax.psum_scatter(phase_real, 'win', scatter_dimension=3, tiled=True)]
    dot_general x6 -> x0, matrix products: 42.6 us -> none  [the longest x5 29.8 us: pair_terms(): jnp.dot(cross.reshape(-1, 2 * bin_count), table, preferred_element_type=j...]
    neg x1 -> x0, other arithmetic: 34.2 us -> none  [transform_table(): return jnp.concatenate([jnp.cos(angle), -jnp.sin(angle)], axis=1)]
    psum x1 -> x0, blocking collectives: 19.7 us -> none  [local(): counts = lax.psum(counts, 'win')]
    pallas_call x0 -> x7, Pallas kernels: none -> 18.1 us  [the longest x3 15.2 us: unit(): pl.pallas_call(functools.partial(unit_kernel, stations, windows, parts, c...]
    reduce_sum x7 -> x0, other arithmetic: 15.5 us -> none  [the longest x5 14.6 us: pair_terms(): linear = jnp.sum(weights[..., None] * real_part, axis=2)]
    ppermute x8 -> x14, starting transfers between devices: 9.28 us -> 22.8 us  [the longest x9 13.4 us: exchange(): lax.ppermute(sums[d], 'win', [(i, i ^ d) for i in range(parts)])]
    sin x1 -> x0, other arithmetic: 8.8 us -> none  [inverse_table(): sine = jnp.sin(angle)]
  transfers between devices with their start and end apart: 11 -> 14, of which waited for: 7 -> 3; matrix products, arithmetic and copies ran while one was open for 4% -> 0% of each run, Pallas kernels for 0% -> 26%
where the time goes in v1:
time: 65.6 us; the launch traced here: 65.3 us
  starting transfers between devices  22.8 us (35%)
  Pallas kernels  18.1 us (28%)
  waiting for transfers between devices  18.1 us (28%)
  local copies, waits for them, and re-layouts  5.24 us (8%)
  other arithmetic  0.78 us (1%)
    pallas_call x3, Pallas kernels, unit(): pl.pallas_call(functools.partial(unit_kernel, stations, windows, parts, c...  15.2 us
    ppermute x9, starting transfers between devices, exchange(): lax.ppermute(sums[d], 'win', [(i, i ^ d) for i in range(parts)])  13.4 us
    ppermute x1, waiting for transfers between devices, local(): lax.ppermute(white, 'sta', [((i + 2) % blocks, i) for i in range(blocks)])  11.2 us
    ppermute x2, waiting for transfers between devices, returned(): return lax.ppermute(value, ('sta', 'win'), route)  6.93 us
    ppermute x2, starting transfers between devices, returned(): return lax.ppermute(value, ('sta', 'win'), route)  5.54 us
    unnamed x20, local copies, waits for them, and re-layouts  5.22 us
    ppermute x1, starting transfers between devices, local(): lax.ppermute(white, 'sta', [((i + 2) % blocks, i) for i in range(blocks)])  3.95 us
    pallas_call x3, Pallas kernels, finish(): pl.pallas_call(functools.partial(finish_kernel, stations, windows, parts,...  1.49 us
  transfers between devices with their start and end apart: 14, of which 3 were waited for; matrix products, arithmetic and copies ran while one was open for 0% of the time, Pallas kernels for 26%

profile of v1, /device:TPU:0, one launch (start us, length us, event | category | flops | bytes accessed | tf_op | source)
XLA Modules:
  0.0 65.3 jit_solution(17460654187716293875)
XLA Ops:
  0.0 0.0 copy-start
  0.0 1.2 %copy-done = f32[8,16,2048]{2,1,0:T(8,128)S(1)} copy-done((f32[8,16,2048]{2,1,0:T(8,128)S(1)}, f32[8,16,2048]{2,1,0:T(8,128)}, u32[]{:S(2)}) %copy-start) | copy-done | bytes 1048600
  1.2 0.0 copy-start.1
  1.2 1.2 %copy-done.1 = bf16[8,256,256]{2,1,0:T(8,128)(2,1)S(1)} copy-done((bf16[8,256,256]{2,1,0:T(8,128)(2,1)S(1)}, bf16[8,256,256]{2,1,0:T(8,128)(2,1)}, u32[]{:S(2)}) %copy-start.1) | copy-done | bytes 1048600
  2.5 0.0 copy-start.2
  2.5 1.2 %copy-done.2 = bf16[8,256,256]{2,1,0:T(8,128)(2,1)S(1)} copy-done((bf16[8,256,256]{2,1,0:T(8,128)(2,1)S(1)}, bf16[8,256,256]{2,1,0:T(8,128)(2,1)}, u32[]{:S(2)}) %copy-start.2) | copy-done | bytes 1048600
  3.7 0.0 copy-start.3
  3.7 0.8 %copy-done.3 = f32[128,128]{1,0:T(8,128)S(1)} copy-done((f32[128,128]{1,0:T(8,128)S(1)}, f32[128,128]{1,0:T(8,128)}, u32[]{:S(2)}) %copy-start.3) | copy-done | bytes 65560
  4.5 0.0 copy-start.4
  4.5 0.7 %copy-done.4 = s32[8,16]{1,0:T(8,128)S(1)} copy-done((s32[8,16]{1,0:T(8,128)S(1)}, s32[8,16]{1,0:T(8,128)}, u32[]{:S(2)}) %copy-start.4) | copy-done | bytes 536
  5.2 0.0 copy-start.5
  5.2 0.0 copy-start.6
  5.2 1.4 %whiten.1.refs_0_.refs_1_ = bf16[128,2048]{1,0:T(8,128)(2,1)S(1)} custom-call(f32[128,2048]{1,0:T(8,128)S(1)} %bitcast.21, s32[8,16]{1,0:T(8,128)S(1)} %copy-done.4, bf16[8,256,256]{2,1,0:T(8,128)(2,1)S(1)} %copy-done.1, bf16[8,256,256]{2,1,0:T(8,128)(2,1)S(1)} %copy-done.2, f32[128,128]{1,0:T(8,128)S(1)} %copy-done.3), custom_call_target="tpu_custom_call" | custom-call | flops 402653184 | bytes 4194304 | tf_op jit(solution)/shard_map/whiten/pallas_call | solution.py:158
  6.6 3.9 %collective-permute-start = (bf16[128,2048]{1,0:T(8,128)(2,1)S(1)}, bf16[128,2048]{1,0:T(8,128)(2,1)S(1)}, u32[]{:S(2)}, u32[]{:S(2)}) collective-permute-start(bf16[128,2048]{1,0:T(8,128)(2,1)S(1)} %whiten.1.refs_0_.refs_1_), channel_id=1, source_target_pairs={{8,0},{12,4},{16,8},{20,12},{24,16},{28,20},{0,24},{4,28},{9,1},{1... | collective-permute-start | bytes 1572872 | tf_op jit(solution)/shard_map/ppermute | solution.py:385
  10.6 0.0 collective-permute-start.5
  10.6 11.2 %collective-permute-done.refs_1_ = bf16[128,2048]{1,0:T(8,128)(2,1)S(1)} collective-permute-done((bf16[128,2048]{1,0:T(8,128)(2,1)S(1)}, bf16[128,2048]{1,0:T(8,128)(2,1)S(1)}, u32[]{:S(2)}, u32[]{:S(2)}) %collective-permute-start) | collective-permute-done | bytes 524320 | tf_op jit(solution)/shard_map/ppermute | solution.py:385
  21.8 0.0 collective-permute-start.6
  21.8 0.0 copy-done.5
  21.8 0.0 copy-done.6
  21.8 5.1 %stack0.1 = (s16[208,128]{1,0:T(8,128)(2,1)S(1)}, s16[208,128]{1,0:T(8,128)(2,1)S(1)}, s16[208,128]{1,0:T(8,128)(2,1)S(1)}, s16[208,128]{1,0:T(8,128)(2,1)S(1)}) custom-call(bf16[128,2048]{1,0:T(8,128)(2,1)S(1)} %whiten.1.refs_0_.refs_1_, bf16[128,2048]{1,0:T(8,128)(2,1)S(1)} %whiten.1.refs_0_.refs_1_, bf16[1024,512]{1,0:T(8,128)(2,1)S(1)} %copy-done.5, ...), custom_call_target="tpu_custom_call" | custom-call | flops 2147483648 | bytes 3145728 | tf_op jit(solution)/shard_map/stack0/pallas_call | solution.py:300
  26.9 1.7 %collective-permute-start.11 = (s16[208,128]{1,0:T(8,128)(2,1)S(1)}, s16[208,128]{1,0:T(8,128)(2,1)S(1)}, u32[]{:S(2)}, u32[]{:S(2)}) collective-permute-start(s16[208,128]{1,0:T(8,128)(2,1)S(1)} %get-tuple-element.32), channel_id=1, source_target_pairs={{0,1},{1,0},{2,3},{3,2},{4,5},{5,4},{6,7},{7,6},{8,9},{9,8},{10,11... | collective-permute-start | bytes 159752 | tf_op jit(solution)/shard_map/ppermute | solution.py:376
  28.5 2.6 %collective-permute-start.12 = (s16[208,128]{1,0:T(8,128)(2,1)S(1)}, s16[208,128]{1,0:T(8,128)(2,1)S(1)}, u32[]{:S(2)}, u32[]{:S(2)}) collective-permute-start(s16[208,128]{1,0:T(8,128)(2,1)S(1)} %get-tuple-element.33), channel_id=1, source_target_pairs={{0,2},{1,3},{2,0},{3,1},{4,6},{5,7},{6,4},{7,5},{8,10},{9,11},{10,... | collective-permute-start | bytes 159752 | tf_op jit(solution)/shard_map/ppermute | solution.py:376
  31.1 0.2 collective-permute-start.13
  31.3 5.1 %stack2.1 = (s16[208,128]{1,0:T(8,128)(2,1)S(1)}, s16[208,128]{1,0:T(8,128)(2,1)S(1)}, s16[208,128]{1,0:T(8,128)(2,1)S(1)}, s16[208,128]{1,0:T(8,128)(2,1)S(1)}) custom-call(bf16[128,2048]{1,0:T(8,128)(2,1)S(1)} %whiten.1.refs_0_.refs_1_, bf16[128,2048]{1,0:T(8,128)(2,1)S(1)} %collective-permute-done.refs_1_, bf16[1024,512]{1,0:T(8,128)(2,1)S(1)} %copy-done.5, ...), custom_call_target="tpu_custom_call" | custom-call | flops 2147483648 | bytes 3145728 | tf_op jit(solution)/shard_map/stack2/pallas_call | solution.py:300
  36.4 0.0 collective-permute-done.11.refs_1_
  36.4 0.8 %collective-permute-start.1 = (s16[208,128]{1,0:T(8,128)(2,1)S(1)}, s16[208,128]{1,0:T(8,128)(2,1)S(1)}, u32[]{:S(2)}, u32[]{:S(2)}) collective-permute-start(s16[208,128]{1,0:T(8,128)(2,1)S(1)} %get-tuple-element.22), channel_id=1, source_target_pairs={{0,1},{1,0},{2,3},{3,2},{4,5},{5,4},{6,7},{7,6},{8,9},{9,8},{10,11... | collective-permute-start | bytes 159752 | tf_op jit(solution)/shard_map/ppermute | solution.py:376
  37.2 0.0 collective-permute-done.5.refs_1_
  37.2 3.5 %collective-permute-start.2 = (s16[208,128]{1,0:T(8,128)(2,1)S(1)}, s16[208,128]{1,0:T(8,128)(2,1)S(1)}, u32[]{:S(2)}, u32[]{:S(2)}) collective-permute-start(s16[208,128]{1,0:T(8,128)(2,1)S(1)} %get-tuple-element.23), channel_id=1, source_target_pairs={{0,2},{1,3},{2,0},{3,1},{4,6},{5,7},{6,4},{7,5},{8,10},{9,11},{10,... | collective-permute-start | bytes 159752 | tf_op jit(solution)/shard_map/ppermute | solution.py:376
  40.7 0.0 collective-permute-done.6.refs_2_
  40.7 0.2 collective-permute-start.3
  40.9 5.1 %stack1.1 = (s16[208,128]{1,0:T(8,128)(2,1)S(1)}, s16[208,128]{1,0:T(8,128)(2,1)S(1)}, s16[208,128]{1,0:T(8,128)(2,1)S(1)}, s16[208,128]{1,0:T(8,128)(2,1)S(1)}) custom-call(bf16[128,2048]{1,0:T(8,128)(2,1)S(1)} %whiten.1.refs_0_.refs_1_, bf16[128,2048]{1,0:T(8,128)(2,1)S(1)} %collective-permute-done.5.refs_1_, ...), custom_call_target="tpu_custom_call" | custom-call | flops 2147483648 | bytes 3145728 | tf_op jit(solution)/shard_map/stack1/pallas_call | solution.py:300
  45.9 0.0 collective-permute-done.1.refs_1_
  45.9 0.5 collective-permute-start.7
  46.5 0.0 collective-permute-done.2.refs_2_
  46.5 3.7 %collective-permute-start.8 = (s16[208,128]{1,0:T(8,128)(2,1)S(1)}, s16[208,128]{1,0:T(8,128)(2,1)S(1)}, u32[]{:S(2)}, u32[]{:S(2)}) collective-permute-start(s16[208,128]{1,0:T(8,128)(2,1)S(1)} %get-tuple-element.28), channel_id=1, source_target_pairs={{0,2},{1,3},{2,0},{3,1},{4,6},{5,7},{6,4},{7,5},{8,10},{9,11},{10,... | collective-permute-start | bytes 159752 | tf_op jit(solution)/shard_map/ppermute | solution.py:376
  50.2 0.0 collective-permute-done.3.refs_3_
  50.2 0.2 collective-permute-start.9
  50.4 0.0 copy-start.7
  50.4 0.5 finish2.1
  50.9 0.0 collective-permute-done.12.refs_2_
  51.0 5.5 %collective-permute-start.4 = (f32[64,128]{1,0:T(8,128)S(1)}, f32[64,128]{1,0:T(8,128)S(1)}, u32[]{:S(2)}, u32[]{:S(2)}) collective-permute-start(f32[64,128]{1,0:T(8,128)S(1)} %get-tuple-element.25), channel_id=1, source_target_pairs={{0,11},{1,10},{2,9},{3,8},{4,15},{5,14},{6,13},{7,12},{8,19},{9,18... | collective-permute-start | bytes 98312 | tf_op jit(solution)/shard_map/ppermute | solution.py:397
  56.5 0.0 copy-done.7
  56.5 0.0 collective-permute-done.13.refs_3_
  56.5 0.4 finish0.1
  56.9 0.0 collective-permute-done.7.refs_1_
  56.9 0.0 collective-permute-done.8.refs_2_
  56.9 0.0 collective-permute-done.9.refs_3_
  57.0 0.5 finish1.1
  57.5 0.0 collective-permute-start.10
  57.5 1.8 %collective-permute-done.4 = f32[64,128]{1,0:T(8,128)S(1)} collective-permute-done((f32[64,128]{1,0:T(8,128)S(1)}, f32[64,128]{1,0:T(8,128)S(1)}, u32[]{:S(2)}, u32[]{:S(2)}) %collective-permute-start.4) | collective-permute-done | bytes 32800 | tf_op jit(solution)/shard_map/ppermute | solution.py:397
  59.3 5.1 %collective-permute-done.10 = f32[64,128]{1,0:T(8,128)S(1)} collective-permute-done((f32[64,128]{1,0:T(8,128)S(1)}, f32[64,128]{1,0:T(8,128)S(1)}, u32[]{:S(2)}, u32[]{:S(2)}) %collective-permute-start.10) | collective-permute-done | bytes 32800 | tf_op jit(solution)/shard_map/ppermute | solution.py:397
  64.5 0.8 %broadcast_multiply_fusion = f32[8,5,8,128]{3,2,1,0:T(8,128)} fusion(f32[8,5,8,128]{3,2,1,0:T(8,128)S(1)} %bitcast_dynamic-update-slice_fusion, f32[8,5,8]{2,1,0:T(8,128)S(1)} %copy.18), kind=kLoop, calls=%fused_computation | loop fusion | flops 40960 | bytes 328960 | tf_op jit(solution)/shard_map/mul | solution.py:408
  (7 shorter events, 0.0 us)
Async XLA Ops:
  0.0 1.2 %copy-start = (f32[8,16,2048]{2,1,0:T(8,128)S(1)}, f32[8,16,2048]{2,1,0:T(8,128)}, u32[]{:S(2)}) copy-start(f32[8,16,2048]{2,1,0:T(8,128)} %param.12) | copy-start | bytes 3145732
  1.2 1.2 %copy-start.1 = (bf16[8,256,256]{2,1,0:T(8,128)(2,1)S(1)}, bf16[8,256,256]{2,1,0:T(8,128)(2,1)}, u32[]{:S(2)}) copy-start(bf16[8,256,256]{2,1,0:T(8,128)(2,1)} %constant.10.clone.high) | copy-start | bytes 3145732
  2.5 1.2 %copy-start.2 = (bf16[8,256,256]{2,1,0:T(8,128)(2,1)S(1)}, bf16[8,256,256]{2,1,0:T(8,128)(2,1)}, u32[]{:S(2)}) copy-start(bf16[8,256,256]{2,1,0:T(8,128)(2,1)} %constant.11.clone.low) | copy-start | bytes 3145732
  3.7 0.8 %copy-start.3 = (f32[128,128]{1,0:T(8,128)S(1)}, f32[128,128]{1,0:T(8,128)}, u32[]{:S(2)}) copy-start(f32[128,128]{1,0:T(8,128)} %constant.12.clone.band) | copy-start | bytes 196612
  4.5 0.7 %copy-start.4 = (s32[8,16]{1,0:T(8,128)S(1)}, s32[8,16]{1,0:T(8,128)}, u32[]{:S(2)}) copy-start(s32[8,16]{1,0:T(8,128)} %gaps.1) | copy-start | bytes 1540
  5.2 16.6 %copy-start.5 = (bf16[1024,512]{1,0:T(8,128)(2,1)S(1)}, bf16[1024,512]{1,0:T(8,128)(2,1)}, u32[]{:S(2)}) copy-start(bf16[1024,512]{1,0:T(8,128)(2,1)} %constant.13.clone.refs_2_.refs_3_) | copy-start | bytes 3145732
  5.2 16.6 %copy-start.6 = (bf16[512,256]{1,0:T(8,128)(2,1)S(1)}, bf16[512,256]{1,0:T(8,128)(2,1)}, u32[]{:S(2)}) copy-start(bf16[512,256]{1,0:T(8,128)(2,1)} %constant.14.clone.refs_3_.refs_4_) | copy-start | bytes 786436
  6.6 15.1 %collective-permute-start = (bf16[128,2048]{1,0:T(8,128)(2,1)S(1)}, bf16[128,2048]{1,0:T(8,128)(2,1)S(1)}, u32[]{:S(2)}, u32[]{:S(2)}) collective-permute-start(bf16[128,2048]{1,0:T(8,128)(2,1)S(1)} %whiten.1.refs_0_.refs_1_), channel_id=1, source_target_pairs={{8,0},{12,4},{16,8},{20,12},{24,16},{28,20},{0,24},{4,28},{9,1},{1... | collective-permute-start | bytes 1572872 | tf_op jit(solution)/shard_map/ppermute | solution.py:385
  10.6 26.6 %collective-permute-start.5 = (bf16[128,2048]{1,0:T(8,128)(2,1)S(1)}, bf16[128,2048]{1,0:T(8,128)(2,1)S(1)}, u32[]{:S(2)}, u32[]{:S(2)}) collective-permute-start(bf16[128,2048]{1,0:T(8,128)(2,1)S(1)} %whiten.1.refs_0_.refs_1_), channel_id=1, source_target_pairs={{4,0},{0,4},{12,8},{8,12},{20,16},{16,20},{28,24},{24,28},{5,1},{1... | collective-permute-start | bytes 1572872 | tf_op jit(solution)/shard_map/ppermute | solution.py:386
  21.8 18.9 %collective-permute-start.6 = (bf16[128,2048]{1,0:T(8,128)(2,1)S(1)}, bf16[128,2048]{1,0:T(8,128)(2,1)S(1)}, u32[]{:S(2)}, u32[]{:S(2)}) collective-permute-start(bf16[128,2048]{1,0:T(8,128)(2,1)S(1)} %collective-permute-done.refs_1_), channel_id=1, source_target_pairs={{4,0},{0,4},{12,8},{8,12},{20,16},{16,20},{28,24},{24,28},{5,1},{1... | collective-permute-start | bytes 1572872 | tf_op jit(solution)/shard_map/ppermute | solution.py:388
  26.9 9.5 %collective-permute-start.11 = (s16[208,128]{1,0:T(8,128)(2,1)S(1)}, s16[208,128]{1,0:T(8,128)(2,1)S(1)}, u32[]{:S(2)}, u32[]{:S(2)}) collective-permute-start(s16[208,128]{1,0:T(8,128)(2,1)S(1)} %get-tuple-element.32), channel_id=1, source_target_pairs={{0,1},{1,0},{2,3},{3,2},{4,5},{5,4},{6,7},{7,6},{8,9},{9,8},{10,11... | collective-permute-start | bytes 159752 | tf_op jit(solution)/shard_map/ppermute | solution.py:376
  28.5 22.4 %collective-permute-start.12 = (s16[208,128]{1,0:T(8,128)(2,1)S(1)}, s16[208,128]{1,0:T(8,128)(2,1)S(1)}, u32[]{:S(2)}, u32[]{:S(2)}) collective-permute-start(s16[208,128]{1,0:T(8,128)(2,1)S(1)} %get-tuple-element.33), channel_id=1, source_target_pairs={{0,2},{1,3},{2,0},{3,1},{4,6},{5,7},{6,4},{7,5},{8,10},{9,11},{10,... | collective-permute-start | bytes 159752 | tf_op jit(solution)/shard_map/ppermute | solution.py:376
  31.1 25.4 %collective-permute-start.13 = (s16[208,128]{1,0:T(8,128)(2,1)S(1)}, s16[208,128]{1,0:T(8,128)(2,1)S(1)}, u32[]{:S(2)}, u32[]{:S(2)}) collective-permute-start(s16[208,128]{1,0:T(8,128)(2,1)S(1)} %get-tuple-element.34), channel_id=1, source_target_pairs={{0,3},{1,2},{2,1},{3,0},{4,7},{5,6},{6,5},{7,4},{8,11},{9,10},{10,... | collective-permute-start | bytes 159752 | tf_op jit(solution)/shard_map/ppermute | solution.py:376
  36.4 9.5 %collective-permute-start.1 = (s16[208,128]{1,0:T(8,128)(2,1)S(1)}, s16[208,128]{1,0:T(8,128)(2,1)S(1)}, u32[]{:S(2)}, u32[]{:S(2)}) collective-permute-start(s16[208,128]{1,0:T(8,128)(2,1)S(1)} %get-tuple-element.22), channel_id=1, source_target_pairs={{0,1},{1,0},{2,3},{3,2},{4,5},{5,4},{6,7},{7,6},{8,9},{9,8},{10,11... | collective-permute-start | bytes 159752 | tf_op jit(solution)/shard_map/ppermute | solution.py:376
  37.2 9.3 %collective-permute-start.2 = (s16[208,128]{1,0:T(8,128)(2,1)S(1)}, s16[208,128]{1,0:T(8,128)(2,1)S(1)}, u32[]{:S(2)}, u32[]{:S(2)}) collective-permute-start(s16[208,128]{1,0:T(8,128)(2,1)S(1)} %get-tuple-element.23), channel_id=1, source_target_pairs={{0,2},{1,3},{2,0},{3,1},{4,6},{5,7},{6,4},{7,5},{8,10},{9,11},{10,... | collective-permute-start | bytes 159752 | tf_op jit(solution)/shard_map/ppermute | solution.py:376
  40.7 9.6 %collective-permute-start.3 = (s16[208,128]{1,0:T(8,128)(2,1)S(1)}, s16[208,128]{1,0:T(8,128)(2,1)S(1)}, u32[]{:S(2)}, u32[]{:S(2)}) collective-permute-start(s16[208,128]{1,0:T(8,128)(2,1)S(1)} %get-tuple-element.24), channel_id=1, source_target_pairs={{0,3},{1,2},{2,1},{3,0},{4,7},{5,6},{6,5},{7,4},{8,11},{9,10},{10,... | collective-permute-start | bytes 159752 | tf_op jit(solution)/shard_map/ppermute | solution.py:376
  45.9 11.0 %collective-permute-start.7 = (s16[208,128]{1,0:T(8,128)(2,1)S(1)}, s16[208,128]{1,0:T(8,128)(2,1)S(1)}, u32[]{:S(2)}, u32[]{:S(2)}) collective-permute-start(s16[208,128]{1,0:T(8,128)(2,1)S(1)} %get-tuple-element.27), channel_id=1, source_target_pairs={{0,1},{1,0},{2,3},{3,2},{4,5},{5,4},{6,7},{7,6},{8,9},{9,8},{10,11... | collective-permute-start | bytes 159752 | tf_op jit(solution)/shard_map/ppermute | solution.py:376
  46.5 10.4 %collective-permute-start.8 = (s16[208,128]{1,0:T(8,128)(2,1)S(1)}, s16[208,128]{1,0:T(8,128)(2,1)S(1)}, u32[]{:S(2)}, u32[]{:S(2)}) collective-permute-start(s16[208,128]{1,0:T(8,128)(2,1)S(1)} %get-tuple-element.28), channel_id=1, source_target_pairs={{0,2},{1,3},{2,0},{3,1},{4,6},{5,7},{6,4},{7,5},{8,10},{9,11},{10,... | collective-permute-start | bytes 159752 | tf_op jit(solution)/shard_map/ppermute | solution.py:376
  50.2 6.7 %collective-permute-start.9 = (s16[208,128]{1,0:T(8,128)(2,1)S(1)}, s16[208,128]{1,0:T(8,128)(2,1)S(1)}, u32[]{:S(2)}, u32[]{:S(2)}) collective-permute-start(s16[208,128]{1,0:T(8,128)(2,1)S(1)} %get-tuple-element.29), channel_id=1, source_target_pairs={{0,3},{1,2},{2,1},{3,0},{4,7},{5,6},{6,5},{7,4},{8,11},{9,10},{10,... | collective-permute-start | bytes 159752 | tf_op jit(solution)/shard_map/ppermute | solution.py:376
  50.4 6.1 %copy-start.7 = (s32[8,5,8]{2,0,1:T(8,128)S(1)}, s32[8,5,8]{2,0,1:T(8,128)}, u32[]{:S(2)}) copy-start(s32[8,5,8]{2,0,1:T(8,128)} %param.14) | copy-start | bytes 3844
  51.0 8.4 %collective-permute-start.4 = (f32[64,128]{1,0:T(8,128)S(1)}, f32[64,128]{1,0:T(8,128)S(1)}, u32[]{:S(2)}, u32[]{:S(2)}) collective-permute-start(f32[64,128]{1,0:T(8,128)S(1)} %get-tuple-element.25), channel_id=1, source_target_pairs={{0,11},{1,10},{2,9},{3,8},{4,15},{5,14},{6,13},{7,12},{8,19},{9,18... | collective-permute-start | bytes 98312 | tf_op jit(solution)/shard_map/ppermute | solution.py:397
  57.5 6.9 %collective-permute-start.10 = (f32[64,128]{1,0:T(8,128)S(1)}, f32[64,128]{1,0:T(8,128)S(1)}, u32[]{:S(2)}, u32[]{:S(2)}) collective-permute-start(f32[64,128]{1,0:T(8,128)S(1)} %get-tuple-element.30), channel_id=1, source_target_pairs={{0,7},{1,6},{2,5},{3,4},{4,11},{5,10},{6,9},{7,8},{8,15},{9,14},{1... | collective-permute-start | bytes 98312 | tf_op jit(solution)/shard_map/ppermute | solution.py:397

commit v2 on v1

--- a/solution.py
+++ b/solution.py
@@ -20,7 +20,7 @@
 HALF = LAGS // 2
 PEAK = 34.0
 EXTRA = 16
-STACK = 4
+STACK = 8
 
 
 def bins():
@@ -31,13 +31,7 @@
     return np.stack(rows)
 
 
-def split(table):
-    high = table.astype(ml_dtypes.bfloat16)
-    low = (table - high.astype(np.float64)).astype(ml_dtypes.bfloat16)
-    return high, low
-
-
-def forward_tables():
+def forward_table():
     at = bins()
     t = np.arange(LANES)
     upper = (np.arange(LANES) >= LANES // 2)[None, :]
@@ -52,12 +46,7 @@
             first = np.concatenate([c, -n], axis=1)
             second = np.concatenate([np.where(upper, -n, n), np.where(upper, -c, c)], axis=1)
         tables.append(np.concatenate([first, second], axis=0))
-    return split(np.stack(tables))
-
-
-def band_table():
-    band = (np.arange(LANES) % (LANES // 2)) // (WBLK // 16)
-    return (band[:, None] == band[None, :]).astype(np.float32)
+    return np.stack(tables).astype(ml_dtypes.bfloat16)
 
 
 def inverse_table():
@@ -108,29 +97,28 @@
     return pairs
 
 
-def forward_kernel(stations, windows, traces, gaps, high, low, band, out, first, second):
+def forward_kernel(stations, windows, signs, flags, table, out, first, second):
     rows = stations * windows
-    block = 16
-    for start in range(0, rows, block):
-        x = traces[start:start + block, :]
-        x = jnp.where(x > 0, 1.0, jnp.where(x < 0, -1.0, 0.0))
+    for start in range(0, rows, 16):
+        x = signs[start:start + 16, :].astype(jnp.float32)
         y = stage_one([x[:, s * LANES:(s + 1) * LANES] for s in range(16)])
         for s in range(SLICES):
             both = jnp.concatenate(y[s], axis=1)
             top = both.astype(jnp.bfloat16)
-            first[s, start:start + block, :] = top
-            second[s, start:start + block, :] = (both - top.astype(jnp.float32)).astype(jnp.bfloat16)
+            first[s, start:start + 16, :] = top
+            second[s, start:start + 16, :] = (both - top.astype(jnp.float32)).astype(jnp.bfloat16)
     spectra = []
     power = jnp.zeros((rows, LANES), jnp.float32)
     for s in range(SLICES):
-        z = jnp.dot(first[s], high[s], preferred_element_type=jnp.float32)
-        z += jnp.dot(second[s], high[s], preferred_element_type=jnp.float32)
-        z += jnp.dot(first[s], low[s], preferred_element_type=jnp.float32)
+        z = jnp.dot(first[s], table[s], preferred_element_type=jnp.float32)
+        z += jnp.dot(second[s], table[s], preferred_element_type=jnp.float32)
         spectra.append(z)
         power += z[:, :LANES] * z[:, :LANES] + z[:, LANES:] * z[:, LANES:]
-    bands = jnp.dot(power, band[...], precision=lax.Precision.HIGHEST, preferred_element_type=jnp.float32)
+    row = lax.broadcasted_iota(jnp.int32, (LANES, LANES), 0) % (LANES // 2) // (WBLK // 16)
+    column = lax.broadcasted_iota(jnp.int32, (LANES, LANES), 1) % (LANES // 2) // (WBLK // 16)
+    band = jnp.where(row == column, 1.0, 0.0)
+    bands = jnp.dot(power, band, precision=lax.Precision.HIGHEST, preferred_element_type=jnp.float32)
     factor = lax.rsqrt(bands * (1.0 / WBLK) + 1e-05)
-    flags = gaps[...].astype(jnp.float32)
     keep = jnp.concatenate(
         [jnp.broadcast_to(flags[:, w:w + 1], (stations, LANES)) for w in range(windows)], axis=0
     )
@@ -154,15 +142,19 @@
 def forward(traces, gaps):
     stations, windows, samples = traces.shape
     rows = stations * windows
-    high, low = forward_tables()
+    signs = jnp.sign(traces.reshape(rows, samples)).astype(jnp.bfloat16)
+    table = jnp.asarray(forward_table()) * lax.optimization_barrier(jnp.ones((), jnp.bfloat16))
     return pl.pallas_call(
         functools.partial(forward_kernel, stations, windows),
         out_shape=jax.ShapeDtypeStruct((rows, 2 * F), jnp.bfloat16),
-        scratch_shapes=[pltpu.VMEM((SLICES, rows, 2 * LANES), jnp.bfloat16)] * 2,
-        compiler_params=pltpu.CompilerParams(vmem_limit_bytes=40 * 1024 * 1024),
+        scratch_shapes=[
+            pltpu.VMEM((SLICES, rows, 2 * LANES), jnp.bfloat16),
+            pltpu.VMEM((SLICES, rows, 2 * LANES), jnp.bfloat16),
+        ],
+        compiler_params=pltpu.CompilerParams(vmem_limit_bytes=16 * 1024 * 1024),
         cost_estimate=pl.CostEstimate(flops=6 * rows * F * 512, bytes_accessed=4 << 20, transcendentals=rows * LANES),
         name="whiten",
-    )(traces.reshape(rows, samples), gaps, jnp.asarray(high), jnp.asarray(low), jnp.asarray(band_table()))
+    )(signs, gaps.astype(jnp.float32), table)
 
 
 def unit_kernel(stations, windows, parts, choose, *refs):
@@ -211,7 +203,7 @@
                 for e in range(2):
                     at = pl.ds((i + e) * stations, stations)
                     counts[at, :] += x0[w, i + e:i + e + 1, :] * y0[w]
-                place = pl.ds(v * pairs + i * stations, 2 * stations)
+                spot = pl.ds(v * pairs + i * stations, 2 * stations)
                 reals, imags = [], []
                 for s in range(SLICES):
                     re = slice(s * LANES, (s + 1) * LANES)
@@ -225,13 +217,13 @@
                     ci = jnp.concatenate([h[1] for h in halves], axis=0)
                     reals.append(cr)
                     imags.append(ci)
-                    cross[0, place, re] = cr.astype(jnp.bfloat16)
-                    cross[1, place, re] = ci.astype(jnp.bfloat16)
+                    cross[0, spot, re] = cr.astype(jnp.bfloat16)
+                    cross[1, spot, re] = ci.astype(jnp.bfloat16)
                 for k, c in enumerate((reals, imags)):
                     cosine = (c[0] - c[4]) + ROOT * ((c[1] + c[7]) - (c[3] + c[5]))
                     sine = (c[2] - c[6]) + ROOT * ((c[1] + c[3]) - (c[5] + c[7]))
-                    fold[place, 2 * k * LANES:(2 * k + 1) * LANES] = cosine.astype(jnp.bfloat16)
-                    fold[place, (2 * k + 1) * LANES:(2 * k + 2) * LANES] = sine.astype(jnp.bfloat16)
+                    fold[spot, 2 * k * LANES:(2 * k + 1) * LANES] = cosine.astype(jnp.bfloat16)
+                    fold[spot, (2 * k + 1) * LANES:(2 * k + 2) * LANES] = sine.astype(jnp.bfloat16)
         from_real = jnp.dot(cross[0], table[...], preferred_element_type=jnp.float32)
         from_imag = jnp.dot(cross[1], table[...], preferred_element_type=jnp.float32)
         rim = jnp.dot(fold[...], edge[...], preferred_element_type=jnp.float32)
@@ -311,7 +303,7 @@
             pltpu.VMEM((3, pairs, LANES), jnp.float32),
             pltpu.VMEM((pairs, LANES), jnp.float32),
         ],
-        compiler_params=pltpu.CompilerParams(vmem_limit_bytes=48 * 1024 * 1024),
+        compiler_params=pltpu.CompilerParams(vmem_limit_bytes=24 * 1024 * 1024),
         cost_estimate=pl.CostEstimate(
             flops=4 * rows * stations * F * LAGS, bytes_accessed=3 << 20, transcendentals=rows * stations * LAGS
         ),
@@ -324,37 +316,40 @@
     outs = refs[parts:]
     pairs = stations * stations
     wide = LAGS // parts
-    me = lax.axis_index("win")
-    acc = sums[0][...].astype(jnp.int32).astype(jnp.float32)
+    negative = lax.axis_index("win") < parts // 2
+    everything = sums[0][...].astype(jnp.int32).astype(jnp.float32)
     for ref in sums[1:]:
-        acc = acc + ref[...].astype(jnp.int32).astype(jnp.float32)
+        everything = everything + ref[...].astype(jnp.int32).astype(jnp.float32)
     scales = (PEAK * windows / 32766.0, windows / 32000.0, windows / 32000.0)
-    tail = jnp.transpose(acc[3 * pairs:])[:pairs]
-    inverse = 1.0 / jnp.maximum(tail[:, 3:4], 1.0)
-
-    def stack(linear, real, imag):
-        linear = linear * scales[0] * inverse
-        real = real * scales[1] * inverse
-        imag = imag * scales[2] * inverse
-        return linear * (real * real + imag * imag)
-
-    plain = stack(acc[:pairs], acc[pairs:2 * pairs], acc[2 * pairs:3 * pairs])
-    edge = stack(tail[:, 0:1], tail[:, 1:2], tail[:, 2:3])
     row = lax.broadcasted_iota(jnp.int32, (LANES, LANES), 0)
     column = lax.broadcasted_iota(jnp.int32, (LANES, LANES), 1)
     mirror = jnp.where((row + column == wide) & (column > 0) & (column < wide), 1.0, 0.0)
-    turned = jnp.dot(plain, mirror, precision=lax.Precision.HIGHEST, preferred_element_type=jnp.float32)
     lane = lax.broadcasted_iota(jnp.int32, (pairs, LANES), 1)
-    turned = jnp.where(lane == 0, edge, turned)
-    negative = me < parts // 2
-    outs[0][...] = jnp.where(negative, turned, plain)
-    if back:
-        value = jnp.where(negative, plain, turned)
-        row = lax.broadcasted_iota(jnp.int32, (pairs, pairs), 0)
-        column = lax.broadcasted_iota(jnp.int32, (pairs, pairs), 1)
-        swap = (row // stations == column % stations) & (row % stations == column // stations)
-        swap = jnp.where(swap, 1.0, 0.0)
-        outs[1][...] = jnp.dot(swap, value, precision=lax.Precision.HIGHEST, preferred_element_type=jnp.float32)
+    row = lax.broadcasted_iota(jnp.int32, (pairs, pairs), 0)
+    column = lax.broadcasted_iota(jnp.int32, (pairs, pairs), 1)
+    swap = (row // stations == column % stations) & (row % stations == column // stations)
+    swap = jnp.where(swap, 1.0, 0.0)
+    if True:
+        acc = everything
+        tail = jnp.transpose(acc[3 * pairs:])[:pairs]
+        inverse = 1.0 / jnp.maximum(tail[:, 3:4], 1.0)
+
+        def stack(linear, real, imag):
+            linear = linear * scales[0] * inverse
+            real = real * scales[1] * inverse
+            imag = imag * scales[2] * inverse
+            return linear * (real * real + imag * imag)
+
+        plain = stack(acc[:pairs], acc[pairs:2 * pairs], acc[2 * pairs:3 * pairs])
+        edge = stack(tail[:, 0:1], tail[:, 1:2], tail[:, 2:3])
+        turned = jnp.dot(plain, mirror, precision=lax.Precision.HIGHEST, preferred_element_type=jnp.float32)
+        turned = jnp.where(lane == 0, edge, turned)
+        outs[0][...] = jnp.where(negative, turned, plain)
+        if back:
+            value = jnp.where(negative, plain, turned)
+            outs[1][...] = jnp.dot(
+                swap, value, precision=lax.Precision.HIGHEST, preferred_element_type=jnp.float32
+            )
 
 
 def finish(stations, windows, sums, back, name):
@@ -384,7 +379,9 @@
     white = forward(traces, gap_mask)
     second = lax.ppermute(white, "sta", [((i + 2) % blocks, i) for i in range(blocks)])
     beside = lax.ppermute(white, "sta", [(i ^ 1, i) for i in range(blocks)])
-    self_sums = exchange(unit(stations, parts, white, [white], "stack0"))
+    own_sums = exchange(unit(stations, parts, white, [white], "stack0"))
+    (middle,) = finish(stations, windows, own_sums, False, "finish0")
+    second, middle = lax.optimization_barrier((second, middle))
     handed = lax.ppermute(second, "sta", [(i ^ 1, i) for i in range(blocks)])
     far_sums = exchange(unit(stations, parts, white, [second], "stack2"))
     near_sums = exchange(unit(stations, parts, white, [beside, handed], "stack1"))
@@ -396,7 +393,6 @@
                 route.append((b * parts + z, ((b + distance) % blocks) * parts + parts - 1 - z))
         return lax.ppermute(value, ("sta", "win"), route)
 
-    (middle,) = finish(stations, windows, self_sums, False, "finish0")
     far, far_back = finish(stations, windows, far_sums, True, "finish2")
     far_back = returned(far_back, 2)
     near, near_back = finish(stations, windows, near_sums, True, "finish1")

time: 65.6 us -> 51.7 us (0.79)
  local copies, waits for them, and re-layouts: 5.24 us -> 0.06 us
  waiting for transfers between devices: 18.1 us -> 14 us
  starting transfers between devices: 22.8 us -> 19 us
  Pallas kernels: 18.1 us -> 15.9 us
  other arithmetic: 0.78 us -> 2.44 us
    ppermute x1, waiting for transfers between devices: 11.2 us -> 0.01 us  [local(): lax.ppermute(white, 'sta', [((i + 2) % blocks, i) for i in range(blocks)])]
    ppermute x9, waiting for transfers between devices: 0.02 us -> 7.07 us  [exchange(): lax.ppermute(sums[d], 'win', [(i, i ^ d) for i in range(parts)])]
    unnamed x20 -> x14, local copies, waits for them, and re-layouts: 5.22 us -> 0.04 us
    ppermute x2, starting transfers between devices: 5.54 us -> 1.64 us  [returned(): return lax.ppermute(value, ('sta', 'win'), route)]
    pallas_call x3, Pallas kernels: 15.2 us -> 13.2 us  [unit(): pl.pallas_call(functools.partial(unit_kernel, stations, windows, parts, c...]
    convert_element_type x0 -> x2, other arithmetic: none -> 1.59 us  [the longest x1 1.58 us: forward(): signs = jnp.sign(traces.reshape(rows, samples)).astype(jnp.bfloat16)]
  transfers between devices with their start and end apart: 14 -> 14, of which waited for: 3 -> 5; matrix products, arithmetic and copies ran while one was open for 0% -> 0% of each run, Pallas kernels for 26% -> 29%
where the time goes in v2:
time: 51.7 us; the launch traced here: 51.5 us
  starting transfers between devices  19 us (37%)
  Pallas kernels  15.9 us (31%)
  waiting for transfers between devices  14 us (27%)
  other arithmetic  2.44 us (5%)
    ppermute x9, starting transfers between devices, exchange(): lax.ppermute(sums[d], 'win', [(i, i ^ d) for i in range(parts)])  13.3 us
    pallas_call x3, Pallas kernels, unit(): pl.pallas_call(functools.partial(unit_kernel, stations, windows, parts, c...  13.2 us
    ppermute x9, waiting for transfers between devices, exchange(): lax.ppermute(sums[d], 'win', [(i, i ^ d) for i in range(parts)])  7.07 us
    ppermute x2, waiting for transfers between devices, returned(): return lax.ppermute(value, ('sta', 'win'), route)  6.88 us
    ppermute x1, starting transfers between devices, local(): lax.ppermute(white, 'sta', [((i + 2) % blocks, i) for i in range(blocks)])  3.95 us
    ppermute x2, starting transfers between devices, returned(): return lax.ppermute(value, ('sta', 'win'), route)  1.64 us
    convert_element_type x1, other arithmetic, forward(): signs = jnp.sign(traces.reshape(rows, samples)).astype(jnp.bfloat16)  1.58 us
    pallas_call x3, Pallas kernels, finish(): pl.pallas_call(functools.partial(finish_kernel, stations, windows, parts,...  1.49 us
  transfers between devices with their start and end apart: 14, of which 5 were waited for; matrix products, arithmetic and copies ran while one was open for 0% of the time, Pallas kernels for 29%

profile of v2, /device:TPU:0, one launch (start us, length us, event | category | flops | bytes accessed | tf_op | source)
XLA Modules:
  0.0 51.5 jit_solution(7105451527498236816)
XLA Ops:
  0.0 0.0 copy-start.2
  0.0 0.0 copy-start.4
  0.0 1.6 %sign_convert_fusion = bf16[8,16,2048]{2,1,0:T(8,128)(2,1)S(1)} fusion(f32[8,16,2048]{2,1,0:T(8,128)} %param.10), kind=kLoop, calls=%fused_computation | loop fusion | flops 524288 | bytes 1572864 | tf_op jit(solution)/shard_map/convert_element_type | solution.py:145
  1.6 0.0 copy-done.4
  1.6 0.0 copy-done.2
  1.6 0.1 broadcast_multiply_fusion.table
  1.7 0.0 copy-start
  1.7 0.0 copy-start.1
  1.7 1.2 %whiten.1.refs_0_.refs_1_ = bf16[128,2048]{1,0:T(8,128)(2,1)S(1)} custom-call(bf16[128,2048]{1,0:T(8,128)(2,1)S(1)} %bitcast.21, f32[8,16]{1,0:T(8,128)S(1)} %convert_element_type.13.flags, bf16[8,256,256]{2,1,0:T(8,128)(2,1)S(1)} %broadcast_multiply_fusion.table), custom_call_target="tpu_custom_call" | custom-call | flops 402653184 | bytes 4194304 | tf_op jit(solution)/shard_map/whiten/pallas_call | solution.py:147
  2.9 3.9 %collective-permute-start = (bf16[128,2048]{1,0:T(8,128)(2,1)S(1)}, bf16[128,2048]{1,0:T(8,128)(2,1)S(1)}, u32[]{:S(2)}, u32[]{:S(2)}) collective-permute-start(bf16[128,2048]{1,0:T(8,128)(2,1)S(1)} %whiten.1.refs_0_.refs_1_), channel_id=1, source_target_pairs={{8,0},{12,4},{16,8},{20,12},{24,16},{28,20},{0,24},{4,28},{9,1},{1... | collective-permute-start | bytes 1572872 | tf_op jit(solution)/shard_map/ppermute | solution.py:380
  6.9 0.0 copy-done
  6.9 0.0 copy-done.1
  6.9 4.4 %stack0.1 = (s16[208,128]{1,0:T(8,128)(2,1)S(1)}, s16[208,128]{1,0:T(8,128)(2,1)S(1)}, s16[208,128]{1,0:T(8,128)(2,1)S(1)}, s16[208,128]{1,0:T(8,128)(2,1)S(1)}) custom-call(bf16[128,2048]{1,0:T(8,128)(2,1)S(1)} %whiten.1.refs_0_.refs_1_, bf16[128,2048]{1,0:T(8,128)(2,1)S(1)} %whiten.1.refs_0_.refs_1_, bf16[1024,512]{1,0:T(8,128)(2,1)S(1)} %copy-done, ...), custom_call_target="tpu_custom_call" | custom-call | flops 2147483648 | bytes 3145728 | tf_op jit(solution)/shard_map/stack0/pallas_call | solution.py:292
  11.3 1.7 %collective-permute-start.1 = (s16[208,128]{1,0:T(8,128)(2,1)S(1)}, s16[208,128]{1,0:T(8,128)(2,1)S(1)}, u32[]{:S(2)}, u32[]{:S(2)}) collective-permute-start(s16[208,128]{1,0:T(8,128)(2,1)S(1)} %get-tuple-element.24), channel_id=1, source_target_pairs={{0,1},{1,0},{2,3},{3,2},{4,5},{5,4},{6,7},{7,6},{8,9},{9,8},{10,11... | collective-permute-start | bytes 159752 | tf_op jit(solution)/shard_map/ppermute | solution.py:371
  13.0 2.6 %collective-permute-start.2 = (s16[208,128]{1,0:T(8,128)(2,1)S(1)}, s16[208,128]{1,0:T(8,128)(2,1)S(1)}, u32[]{:S(2)}, u32[]{:S(2)}) collective-permute-start(s16[208,128]{1,0:T(8,128)(2,1)S(1)} %get-tuple-element.25), channel_id=1, source_target_pairs={{0,2},{1,3},{2,0},{3,1},{4,6},{5,7},{6,4},{7,5},{8,10},{9,11},{10,... | collective-permute-start | bytes 159752 | tf_op jit(solution)/shard_map/ppermute | solution.py:371
  15.5 0.2 collective-permute-start.3
  15.7 0.0 collective-permute-start.8
  15.7 0.0 collective-permute-done.1.refs_1_
  15.8 3.0 %collective-permute-done.2.refs_2_ = s16[208,128]{1,0:T(8,128)(2,1)S(1)} collective-permute-done((s16[208,128]{1,0:T(8,128)(2,1)S(1)}, s16[208,128]{1,0:T(8,128)(2,1)S(1)}, u32[]{:S(2)}, u32[]{:S(2)}) %collective-permute-start.2) | collective-permute-done | bytes 53280 | tf_op jit(solution)/shard_map/ppermute | solution.py:371
  18.7 2.7 %collective-permute-done.3.refs_3_ = s16[208,128]{1,0:T(8,128)(2,1)S(1)} collective-permute-done((s16[208,128]{1,0:T(8,128)(2,1)S(1)}, s16[208,128]{1,0:T(8,128)(2,1)S(1)}, u32[]{:S(2)}, u32[]{:S(2)}) %collective-permute-start.3) | collective-permute-done | bytes 53280 | tf_op jit(solution)/shard_map/ppermute | solution.py:371
  21.5 0.4 finish0.1
  21.9 0.0 collective-permute-done.refs_1_
  21.9 0.1 collective-permute-start.9
  22.0 4.4 %stack2.1 = (s16[208,128]{1,0:T(8,128)(2,1)S(1)}, s16[208,128]{1,0:T(8,128)(2,1)S(1)}, s16[208,128]{1,0:T(8,128)(2,1)S(1)}, s16[208,128]{1,0:T(8,128)(2,1)S(1)}) custom-call(bf16[128,2048]{1,0:T(8,128)(2,1)S(1)} %whiten.1.refs_0_.refs_1_, bf16[128,2048]{1,0:T(8,128)(2,1)S(1)} %collective-permute-done.refs_1_, bf16[1024,512]{1,0:T(8,128)(2,1)S(1)} %copy-done, ...), custom_call_target="tpu_custom_call" | custom-call | flops 2147483648 | bytes 3145728 | tf_op jit(solution)/shard_map/stack2/pallas_call | solution.py:292
  26.4 0.1 collective-permute-start.4
  26.4 1.3 %collective-permute-start.5 = (s16[208,128]{1,0:T(8,128)(2,1)S(1)}, s16[208,128]{1,0:T(8,128)(2,1)S(1)}, u32[]{:S(2)}, u32[]{:S(2)}) collective-permute-start(s16[208,128]{1,0:T(8,128)(2,1)S(1)} %get-tuple-element.30), channel_id=1, source_target_pairs={{0,2},{1,3},{2,0},{3,1},{4,6},{5,7},{6,4},{7,5},{8,10},{9,11},{10,... | collective-permute-start | bytes 159752 | tf_op jit(solution)/shard_map/ppermute | solution.py:371
  27.7 3.1 %collective-permute-start.6 = (s16[208,128]{1,0:T(8,128)(2,1)S(1)}, s16[208,128]{1,0:T(8,128)(2,1)S(1)}, u32[]{:S(2)}, u32[]{:S(2)}) collective-permute-start(s16[208,128]{1,0:T(8,128)(2,1)S(1)} %get-tuple-element.31), channel_id=1, source_target_pairs={{0,3},{1,2},{2,1},{3,0},{4,7},{5,6},{6,5},{7,4},{8,11},{9,10},{10,... | collective-permute-start | bytes 159752 | tf_op jit(solution)/shard_map/ppermute | solution.py:371
  30.8 0.0 collective-permute-done.8.refs_1_
  30.8 0.0 collective-permute-done.9.refs_2_
  30.8 4.4 %stack1.1 = (s16[208,128]{1,0:T(8,128)(2,1)S(1)}, s16[208,128]{1,0:T(8,128)(2,1)S(1)}, s16[208,128]{1,0:T(8,128)(2,1)S(1)}, s16[208,128]{1,0:T(8,128)(2,1)S(1)}) custom-call(bf16[128,2048]{1,0:T(8,128)(2,1)S(1)} %whiten.1.refs_0_.refs_1_, bf16[128,2048]{1,0:T(8,128)(2,1)S(1)} %collective-permute-done.8.refs_1_, ...), custom_call_target="tpu_custom_call" | custom-call | flops 2147483648 | bytes 3145728 | tf_op jit(solution)/shard_map/stack1/pallas_call | solution.py:292
  35.2 0.1 collective-permute-start.10
  35.3 1.3 %collective-permute-start.11 = (s16[208,128]{1,0:T(8,128)(2,1)S(1)}, s16[208,128]{1,0:T(8,128)(2,1)S(1)}, u32[]{:S(2)}, u32[]{:S(2)}) collective-permute-start(s16[208,128]{1,0:T(8,128)(2,1)S(1)} %get-tuple-element.35), channel_id=1, source_target_pairs={{0,2},{1,3},{2,0},{3,1},{4,6},{5,7},{6,4},{7,5},{8,10},{9,11},{10,... | collective-permute-start | bytes 159752 | tf_op jit(solution)/shard_map/ppermute | solution.py:371
  36.6 0.0 collective-permute-done.4.refs_1_
  36.6 3.1 %collective-permute-start.12 = (s16[208,128]{1,0:T(8,128)(2,1)S(1)}, s16[208,128]{1,0:T(8,128)(2,1)S(1)}, u32[]{:S(2)}, u32[]{:S(2)}) collective-permute-start(s16[208,128]{1,0:T(8,128)(2,1)S(1)} %get-tuple-element.36), channel_id=1, source_target_pairs={{0,3},{1,2},{2,1},{3,0},{4,7},{5,6},{6,5},{7,4},{8,11},{9,10},{10,... | collective-permute-start | bytes 159752 | tf_op jit(solution)/shard_map/ppermute | solution.py:371
  39.7 0.0 collective-permute-done.5.refs_2_
  39.7 0.0 collective-permute-done.6.refs_3_
  39.7 0.0 copy-start.3
  39.7 0.5 %finish2.1 = (f32[64,128]{1,0:T(8,128)S(1)}, f32[64,128]{1,0:T(8,128)S(1)}) custom-call(s16[208,128]{1,0:T(8,128)(2,1)S(1)} %get-tuple-element.28.refs_0_, s16[208,128]{1,0:T(8,128)(2,1)S(1)} %collective-permute-done.4.refs_1_, s16[208,128]{1,0:T(8,128)(2,1)S(1)} %collective-permute-done.5.refs_2_, s16[208,128]{1,0:T(8,128)(2,1)S(1)} %collective-permute-done.6.refs_3_), custom_call_target="tpu_custom_call" | custom-call | flops 4194304 | bytes 262144 | tf_op jit(solution)/shard_map/finish2/pallas_call | solution.py:359
  40.3 1.6 %collective-permute-start.7 = (f32[64,128]{1,0:T(8,128)S(1)}, f32[64,128]{1,0:T(8,128)S(1)}, u32[]{:S(2)}, u32[]{:S(2)}) collective-permute-start(f32[64,128]{1,0:T(8,128)S(1)} %get-tuple-element.32), channel_id=1, source_target_pairs={{0,11},{1,10},{2,9},{3,8},{4,15},{5,14},{6,13},{7,12},{8,19},{9,18... | collective-permute-start | bytes 98312 | tf_op jit(solution)/shard_map/ppermute | solution.py:394
  41.9 0.0 copy-done.3
  41.9 0.0 collective-permute-done.10.refs_1_
  41.9 1.3 %collective-permute-done.11.refs_2_ = s16[208,128]{1,0:T(8,128)(2,1)S(1)} collective-permute-done((s16[208,128]{1,0:T(8,128)(2,1)S(1)}, s16[208,128]{1,0:T(8,128)(2,1)S(1)}, u32[]{:S(2)}, u32[]{:S(2)}) %collective-permute-start.11) | collective-permute-done | bytes 53280 | tf_op jit(solution)/shard_map/ppermute | solution.py:371
  43.2 0.0 collective-permute-done.12.refs_3_
  43.2 0.5 %finish1.1 = (f32[64,128]{1,0:T(8,128)S(1)}, f32[64,128]{1,0:T(8,128)S(1)}) custom-call(s16[208,128]{1,0:T(8,128)(2,1)S(1)} %get-tuple-element.33.refs_0_, s16[208,128]{1,0:T(8,128)(2,1)S(1)} %collective-permute-done.10.refs_1_, s16[208,128]{1,0:T(8,128)(2,1)S(1)} %collective-permute-done.11.refs_2_, s16[208,128]{1,0:T(8,128)(2,1)S(1)} %collective-permute-done.12.refs_3_), custom_call_target="tpu_custom_call" | custom-call | flops 4194304 | bytes 262144 | tf_op jit(solution)/shard_map/finish1/pallas_call | solution.py:359
  43.8 0.1 collective-permute-start.13
  43.8 4.1 %collective-permute-done.7 = f32[64,128]{1,0:T(8,128)S(1)} collective-permute-done((f32[64,128]{1,0:T(8,128)S(1)}, f32[64,128]{1,0:T(8,128)S(1)}, u32[]{:S(2)}, u32[]{:S(2)}) %collective-permute-start.7) | collective-permute-done | bytes 32800 | tf_op jit(solution)/shard_map/ppermute | solution.py:394
  47.9 2.8 %collective-permute-done.13 = f32[64,128]{1,0:T(8,128)S(1)} collective-permute-done((f32[64,128]{1,0:T(8,128)S(1)}, f32[64,128]{1,0:T(8,128)S(1)}, u32[]{:S(2)}, u32[]{:S(2)}) %collective-permute-start.13) | collective-permute-done | bytes 32800 | tf_op jit(solution)/shard_map/ppermute | solution.py:394
  50.8 0.8 %broadcast_multiply_fusion.1 = f32[8,5,8,128]{3,2,1,0:T(8,128)} fusion(f32[8,5,8,128]{3,2,1,0:T(8,128)S(1)} %bitcast_dynamic-update-slice_fusion, f32[8,5,8]{2,1,0:T(8,128)S(1)} %copy.16), kind=kLoop, calls=%fused_computation.2 | loop fusion | flops 40960 | bytes 328960 | tf_op jit(solution)/shard_map/mul | solution.py:404
  (8 shorter events, 0.0 us)
Async XLA Ops:
  0.0 1.6 %copy-start.2 = (bf16[8,256,256]{2,1,0:T(8,128)(2,1)S(1)}, bf16[8,256,256]{2,1,0:T(8,128)(2,1)}, u32[]{:S(2)}) copy-start(bf16[8,256,256]{2,1,0:T(8,128)(2,1)} %constant.8.clone) | copy-start | bytes 3145732
  0.0 1.6 %copy-start.4 = (s32[8,16]{1,0:T(8,128)S(1)}, s32[8,16]{1,0:T(8,128)}, u32[]{:S(2)}) copy-start(s32[8,16]{1,0:T(8,128)} %param.11) | copy-start | bytes 1540
  1.7 5.2 %copy-start = (bf16[1024,512]{1,0:T(8,128)(2,1)S(1)}, bf16[1024,512]{1,0:T(8,128)(2,1)}, u32[]{:S(2)}) copy-start(bf16[1024,512]{1,0:T(8,128)(2,1)} %constant.9.clone.refs_2_.refs_3_) | copy-start | bytes 3145732
  1.7 5.2 %copy-start.1 = (bf16[512,256]{1,0:T(8,128)(2,1)S(1)}, bf16[512,256]{1,0:T(8,128)(2,1)}, u32[]{:S(2)}) copy-start(bf16[512,256]{1,0:T(8,128)(2,1)} %constant.10.clone.refs_3_.refs_4_) | copy-start | bytes 786436
  2.9 18.9 %collective-permute-start = (bf16[128,2048]{1,0:T(8,128)(2,1)S(1)}, bf16[128,2048]{1,0:T(8,128)(2,1)S(1)}, u32[]{:S(2)}, u32[]{:S(2)}) collective-permute-start(bf16[128,2048]{1,0:T(8,128)(2,1)S(1)} %whiten.1.refs_0_.refs_1_), channel_id=1, source_target_pairs={{8,0},{12,4},{16,8},{20,12},{24,16},{28,20},{0,24},{4,28},{9,1},{1... | collective-permute-start | bytes 1572872 | tf_op jit(solution)/shard_map/ppermute | solution.py:380
  11.3 4.5 %collective-permute-start.1 = (s16[208,128]{1,0:T(8,128)(2,1)S(1)}, s16[208,128]{1,0:T(8,128)(2,1)S(1)}, u32[]{:S(2)}, u32[]{:S(2)}) collective-permute-start(s16[208,128]{1,0:T(8,128)(2,1)S(1)} %get-tuple-element.24), channel_id=1, source_target_pairs={{0,1},{1,0},{2,3},{3,2},{4,5},{5,4},{6,7},{7,6},{8,9},{9,8},{10,11... | collective-permute-start | bytes 159752 | tf_op jit(solution)/shard_map/ppermute | solution.py:371
  13.0 5.8 %collective-permute-start.2 = (s16[208,128]{1,0:T(8,128)(2,1)S(1)}, s16[208,128]{1,0:T(8,128)(2,1)S(1)}, u32[]{:S(2)}, u32[]{:S(2)}) collective-permute-start(s16[208,128]{1,0:T(8,128)(2,1)S(1)} %get-tuple-element.25), channel_id=1, source_target_pairs={{0,2},{1,3},{2,0},{3,1},{4,6},{5,7},{6,4},{7,5},{8,10},{9,11},{10,... | collective-permute-start | bytes 159752 | tf_op jit(solution)/shard_map/ppermute | solution.py:371
  15.5 5.9 %collective-permute-start.3 = (s16[208,128]{1,0:T(8,128)(2,1)S(1)}, s16[208,128]{1,0:T(8,128)(2,1)S(1)}, u32[]{:S(2)}, u32[]{:S(2)}) collective-permute-start(s16[208,128]{1,0:T(8,128)(2,1)S(1)} %get-tuple-element.26), channel_id=1, source_target_pairs={{0,3},{1,2},{2,1},{3,0},{4,7},{5,6},{6,5},{7,4},{8,11},{9,10},{10,... | collective-permute-start | bytes 159752 | tf_op jit(solution)/shard_map/ppermute | solution.py:371
  15.7 15.1 %collective-permute-start.8 = (bf16[128,2048]{1,0:T(8,128)(2,1)S(1)}, bf16[128,2048]{1,0:T(8,128)(2,1)S(1)}, u32[]{:S(2)}, u32[]{:S(2)}) collective-permute-start(bf16[128,2048]{1,0:T(8,128)(2,1)S(1)} %whiten.1.refs_0_.refs_1_), channel_id=1, source_target_pairs={{4,0},{0,4},{12,8},{8,12},{20,16},{16,20},{28,24},{24,28},{5,1},{1... | collective-permute-start | bytes 1572872 | tf_op jit(solution)/shard_map/ppermute | solution.py:381
  21.9 9.0 %collective-permute-start.9 = (bf16[128,2048]{1,0:T(8,128)(2,1)S(1)}, bf16[128,2048]{1,0:T(8,128)(2,1)S(1)}, u32[]{:S(2)}, u32[]{:S(2)}) collective-permute-start(bf16[128,2048]{1,0:T(8,128)(2,1)S(1)} %collective-permute-done.refs_1_), channel_id=1, source_target_pairs={{4,0},{0,4},{12,8},{8,12},{20,16},{16,20},{28,24},{24,28},{5,1},{1... | collective-permute-start | bytes 1572872 | tf_op jit(solution)/shard_map/ppermute | solution.py:385
  26.4 10.2 %collective-permute-start.4 = (s16[208,128]{1,0:T(8,128)(2,1)S(1)}, s16[208,128]{1,0:T(8,128)(2,1)S(1)}, u32[]{:S(2)}, u32[]{:S(2)}) collective-permute-start(s16[208,128]{1,0:T(8,128)(2,1)S(1)} %get-tuple-element.29), channel_id=1, source_target_pairs={{0,1},{1,0},{2,3},{3,2},{4,5},{5,4},{6,7},{7,6},{8,9},{9,8},{10,11... | collective-permute-start | bytes 159752 | tf_op jit(solution)/shard_map/ppermute | solution.py:371
  26.4 13.3 %collective-permute-start.5 = (s16[208,128]{1,0:T(8,128)(2,1)S(1)}, s16[208,128]{1,0:T(8,128)(2,1)S(1)}, u32[]{:S(2)}, u32[]{:S(2)}) collective-permute-start(s16[208,128]{1,0:T(8,128)(2,1)S(1)} %get-tuple-element.30), channel_id=1, source_target_pairs={{0,2},{1,3},{2,0},{3,1},{4,6},{5,7},{6,4},{7,5},{8,10},{9,11},{10,... | collective-permute-start | bytes 159752 | tf_op jit(solution)/shard_map/ppermute | solution.py:371
  27.7 12.0 %collective-permute-start.6 = (s16[208,128]{1,0:T(8,128)(2,1)S(1)}, s16[208,128]{1,0:T(8,128)(2,1)S(1)}, u32[]{:S(2)}, u32[]{:S(2)}) collective-permute-start(s16[208,128]{1,0:T(8,128)(2,1)S(1)} %get-tuple-element.31), channel_id=1, source_target_pairs={{0,3},{1,2},{2,1},{3,0},{4,7},{5,6},{6,5},{7,4},{8,11},{9,10},{10,... | collective-permute-start | bytes 159752 | tf_op jit(solution)/shard_map/ppermute | solution.py:371
  35.2 6.6 %collective-permute-start.10 = (s16[208,128]{1,0:T(8,128)(2,1)S(1)}, s16[208,128]{1,0:T(8,128)(2,1)S(1)}, u32[]{:S(2)}, u32[]{:S(2)}) collective-permute-start(s16[208,128]{1,0:T(8,128)(2,1)S(1)} %get-tuple-element.34), channel_id=1, source_target_pairs={{0,1},{1,0},{2,3},{3,2},{4,5},{5,4},{6,7},{7,6},{8,9},{9,8},{10,11... | collective-permute-start | bytes 159752 | tf_op jit(solution)/shard_map/ppermute | solution.py:371
  35.3 7.9 %collective-permute-start.11 = (s16[208,128]{1,0:T(8,128)(2,1)S(1)}, s16[208,128]{1,0:T(8,128)(2,1)S(1)}, u32[]{:S(2)}, u32[]{:S(2)}) collective-permute-start(s16[208,128]{1,0:T(8,128)(2,1)S(1)} %get-tuple-element.35), channel_id=1, source_target_pairs={{0,2},{1,3},{2,0},{3,1},{4,6},{5,7},{6,4},{7,5},{8,10},{9,11},{10,... | collective-permute-start | bytes 159752 | tf_op jit(solution)/shard_map/ppermute | solution.py:371
  36.6 6.6 %collective-permute-start.12 = (s16[208,128]{1,0:T(8,128)(2,1)S(1)}, s16[208,128]{1,0:T(8,128)(2,1)S(1)}, u32[]{:S(2)}, u32[]{:S(2)}) collective-permute-start(s16[208,128]{1,0:T(8,128)(2,1)S(1)} %get-tuple-element.36), channel_id=1, source_target_pairs={{0,3},{1,2},{2,1},{3,0},{4,7},{5,6},{6,5},{7,4},{8,11},{9,10},{10,... | collective-permute-start | bytes 159752 | tf_op jit(solution)/shard_map/ppermute | solution.py:371
  39.7 2.1 %copy-start.3 = (s32[8,5,8]{2,0,1:T(8,128)S(1)}, s32[8,5,8]{2,0,1:T(8,128)}, u32[]{:S(2)}) copy-start(s32[8,5,8]{2,0,1:T(8,128)} %param.12) | copy-start | bytes 3844
  40.3 7.6 %collective-permute-start.7 = (f32[64,128]{1,0:T(8,128)S(1)}, f32[64,128]{1,0:T(8,128)S(1)}, u32[]{:S(2)}, u32[]{:S(2)}) collective-permute-start(f32[64,128]{1,0:T(8,128)S(1)} %get-tuple-element.32), channel_id=1, source_target_pairs={{0,11},{1,10},{2,9},{3,8},{4,15},{5,14},{6,13},{7,12},{8,19},{9,18... | collective-permute-start | bytes 98312 | tf_op jit(solution)/shard_map/ppermute | solution.py:394
  43.8 6.9 %collective-permute-start.13 = (f32[64,128]{1,0:T(8,128)S(1)}, f32[64,128]{1,0:T(8,128)S(1)}, u32[]{:S(2)}, u32[]{:S(2)}) collective-permute-start(f32[64,128]{1,0:T(8,128)S(1)} %get-tuple-element.37), channel_id=1, source_target_pairs={{0,7},{1,6},{2,5},{3,4},{4,11},{5,10},{6,9},{7,8},{8,15},{9,14},{1... | collective-permute-start | bytes 98312 | tf_op jit(solution)/shard_map/ppermute | solution.py:394

commit v3 on v2

--- a/solution.py
+++ b/solution.py
@@ -20,7 +20,7 @@
 HALF = LAGS // 2
 PEAK = 34.0
 EXTRA = 16
-STACK = 8
+STACK = 16
 
 
 def bins():
@@ -368,7 +368,7 @@
 def exchange(sums):
     parts = len(sums)
     return [sums[0]] + [
-        lax.ppermute(sums[d], "win", [(i, i ^ d) for i in range(parts)]) for d in range(1, parts)
+        lax.ppermute(sums[d], "win", [(i, i ^ d) for i in range(parts)]) for d in range(parts - 1, 0, -1)
     ]
 
 

time: 51.7 us -> 50.3 us (0.973)
  waiting for transfers between devices: 14 us -> 10.9 us
  starting transfers between devices: 19 us -> 20.9 us
    ppermute x9, waiting for transfers between devices: 7.07 us -> 4.27 us  [exchange(): lax.ppermute(sums[d], 'win', [(i, i ^ d) for i in range(parts)])]
    ppermute x2, starting transfers between devices: 1.64 us -> 3.57 us  [returned(): return lax.ppermute(value, ('sta', 'win'), route)]
  transfers between devices with their start and end apart: 14 -> 14, of which waited for: 5 -> 4; matrix products, arithmetic and copies ran while one was open for 0% -> 0% of each run, Pallas kernels for 29% -> 29%
where the time goes in v3:
time: 50.3 us; the launch traced here: 50.1 us
  starting transfers between devices  20.9 us (42%)
  Pallas kernels  15.6 us (31%)
  waiting for transfers between devices  10.9 us (22%)
  other arithmetic  2.44 us (5%)
    ppermute x9, starting transfers between devices, exchange(): lax.ppermute(sums[d], 'win', [(i, i ^ d) for i in range(parts)])  13.4 us
    pallas_call x3, Pallas kernels, unit(): pl.pallas_call(functools.partial(unit_kernel, stations, windows, parts, c...  12.9 us
    ppermute x2, waiting for transfers between devices, returned(): return lax.ppermute(value, ('sta', 'win'), route)  6.64 us
    ppermute x9, waiting for transfers between devices, exchange(): lax.ppermute(sums[d], 'win', [(i, i ^ d) for i in range(parts)])  4.27 us
    ppermute x1, starting transfers between devices, local(): lax.ppermute(white, 'sta', [((i + 2) % blocks, i) for i in range(blocks)])  3.95 us
    ppermute x2, starting transfers between devices, returned(): return lax.ppermute(value, ('sta', 'win'), route)  3.57 us
    convert_element_type x1, other arithmetic, forward(): signs = jnp.sign(traces.reshape(rows, samples)).astype(jnp.bfloat16)  1.58 us
    pallas_call x3, Pallas kernels, finish(): pl.pallas_call(functools.partial(finish_kernel, stations, windows, parts,...  1.49 us
  transfers between devices with their start and end apart: 14, of which 4 were waited for; matrix products, arithmetic and copies ran while one was open for 0% of the time, Pallas kernels for 29%

profile of v3, /device:TPU:0, one launch (start us, length us, event | category | flops | bytes accessed | tf_op | source)
XLA Modules:
  0.0 50.1 jit_solution(10134436347690135480)
XLA Ops:
  0.0 0.0 copy-start.2
  0.0 0.0 copy-start.4
  0.0 1.6 %sign_convert_fusion = bf16[8,16,2048]{2,1,0:T(8,128)(2,1)S(1)} fusion(f32[8,16,2048]{2,1,0:T(8,128)} %param.10), kind=kLoop, calls=%fused_computation | loop fusion | flops 524288 | bytes 1572864 | tf_op jit(solution)/shard_map/convert_element_type | solution.py:145
  1.6 0.0 copy-done.4
  1.6 0.0 copy-done.2
  1.6 0.1 broadcast_multiply_fusion.table
  1.7 0.0 copy-start
  1.7 0.0 copy-start.1
  1.7 1.2 %whiten.1.refs_0_.refs_1_ = bf16[128,2048]{1,0:T(8,128)(2,1)S(1)} custom-call(bf16[128,2048]{1,0:T(8,128)(2,1)S(1)} %bitcast.21, f32[8,16]{1,0:T(8,128)S(1)} %convert_element_type.13.flags, bf16[8,256,256]{2,1,0:T(8,128)(2,1)S(1)} %broadcast_multiply_fusion.table), custom_call_target="tpu_custom_call" | custom-call | flops 402653184 | bytes 4194304 | tf_op jit(solution)/shard_map/whiten/pallas_call | solution.py:147
  2.9 3.9 %collective-permute-start = (bf16[128,2048]{1,0:T(8,128)(2,1)S(1)}, bf16[128,2048]{1,0:T(8,128)(2,1)S(1)}, u32[]{:S(2)}, u32[]{:S(2)}) collective-permute-start(bf16[128,2048]{1,0:T(8,128)(2,1)S(1)} %whiten.1.refs_0_.refs_1_), channel_id=1, source_target_pairs={{8,0},{12,4},{16,8},{20,12},{24,16},{28,20},{0,24},{4,28},{9,1},{1... | collective-permute-start | bytes 1572872 | tf_op jit(solution)/shard_map/ppermute | solution.py:380
  6.9 0.0 copy-done
  6.9 0.0 copy-done.1
  6.9 4.2 %stack0.1 = (s16[208,128]{1,0:T(8,128)(2,1)S(1)}, s16[208,128]{1,0:T(8,128)(2,1)S(1)}, s16[208,128]{1,0:T(8,128)(2,1)S(1)}, s16[208,128]{1,0:T(8,128)(2,1)S(1)}) custom-call(bf16[128,2048]{1,0:T(8,128)(2,1)S(1)} %whiten.1.refs_0_.refs_1_, bf16[128,2048]{1,0:T(8,128)(2,1)S(1)} %whiten.1.refs_0_.refs_1_, bf16[1024,512]{1,0:T(8,128)(2,1)S(1)} %copy-done, ...), custom_call_target="tpu_custom_call" | custom-call | flops 2147483648 | bytes 3145728 | tf_op jit(solution)/shard_map/stack0/pallas_call | solution.py:292
  11.1 3.7 %collective-permute-start.1 = (s16[208,128]{1,0:T(8,128)(2,1)S(1)}, s16[208,128]{1,0:T(8,128)(2,1)S(1)}, u32[]{:S(2)}, u32[]{:S(2)}) collective-permute-start(s16[208,128]{1,0:T(8,128)(2,1)S(1)} %get-tuple-element.24), channel_id=1, source_target_pairs={{0,3},{1,2},{2,1},{3,0},{4,7},{5,6},{6,5},{7,4},{8,11},{9,10},{10,... | collective-permute-start | bytes 159752 | tf_op jit(solution)/shard_map/ppermute | solution.py:371
  14.8 0.0 collective-permute-start.2
  14.8 0.8 %collective-permute-start.3 = (s16[208,128]{1,0:T(8,128)(2,1)S(1)}, s16[208,128]{1,0:T(8,128)(2,1)S(1)}, u32[]{:S(2)}, u32[]{:S(2)}) collective-permute-start(s16[208,128]{1,0:T(8,128)(2,1)S(1)} %get-tuple-element.26), channel_id=1, source_target_pairs={{0,1},{1,0},{2,3},{3,2},{4,5},{5,4},{6,7},{7,6},{8,9},{9,8},{10,11... | collective-permute-start | bytes 159752 | tf_op jit(solution)/shard_map/ppermute | solution.py:371
  15.5 0.0 collective-permute-start.8
  15.5 2.2 %collective-permute-done.1.refs_1_ = s16[208,128]{1,0:T(8,128)(2,1)S(1)} collective-permute-done((s16[208,128]{1,0:T(8,128)(2,1)S(1)}, s16[208,128]{1,0:T(8,128)(2,1)S(1)}, u32[]{:S(2)}, u32[]{:S(2)}) %collective-permute-start.1) | collective-permute-done | bytes 53280 | tf_op jit(solution)/shard_map/ppermute | solution.py:371
  17.7 2.1 %collective-permute-done.2.refs_2_ = s16[208,128]{1,0:T(8,128)(2,1)S(1)} collective-permute-done((s16[208,128]{1,0:T(8,128)(2,1)S(1)}, s16[208,128]{1,0:T(8,128)(2,1)S(1)}, u32[]{:S(2)}, u32[]{:S(2)}) %collective-permute-start.2) | collective-permute-done | bytes 53280 | tf_op jit(solution)/shard_map/ppermute | solution.py:371
  19.8 0.0 collective-permute-done.3.refs_3_
  19.8 0.4 finish0.1
  20.2 0.0 collective-permute-done.refs_1_
  20.2 0.1 collective-permute-start.9
  20.3 4.2 %stack2.1 = (s16[208,128]{1,0:T(8,128)(2,1)S(1)}, s16[208,128]{1,0:T(8,128)(2,1)S(1)}, s16[208,128]{1,0:T(8,128)(2,1)S(1)}, s16[208,128]{1,0:T(8,128)(2,1)S(1)}) custom-call(bf16[128,2048]{1,0:T(8,128)(2,1)S(1)} %whiten.1.refs_0_.refs_1_, bf16[128,2048]{1,0:T(8,128)(2,1)S(1)} %collective-permute-done.refs_1_, bf16[1024,512]{1,0:T(8,128)(2,1)S(1)} %copy-done, ...), custom_call_target="tpu_custom_call" | custom-call | flops 2147483648 | bytes 3145728 | tf_op jit(solution)/shard_map/stack2/pallas_call | solution.py:292
  24.5 2.2 %collective-permute-start.4 = (s16[208,128]{1,0:T(8,128)(2,1)S(1)}, s16[208,128]{1,0:T(8,128)(2,1)S(1)}, u32[]{:S(2)}, u32[]{:S(2)}) collective-permute-start(s16[208,128]{1,0:T(8,128)(2,1)S(1)} %get-tuple-element.29), channel_id=1, source_target_pairs={{0,3},{1,2},{2,1},{3,0},{4,7},{5,6},{6,5},{7,4},{8,11},{9,10},{10,... | collective-permute-start | bytes 159752 | tf_op jit(solution)/shard_map/ppermute | solution.py:371
  26.6 0.0 collective-permute-start.5
  26.7 2.3 %collective-permute-start.6 = (s16[208,128]{1,0:T(8,128)(2,1)S(1)}, s16[208,128]{1,0:T(8,128)(2,1)S(1)}, u32[]{:S(2)}, u32[]{:S(2)}) collective-permute-start(s16[208,128]{1,0:T(8,128)(2,1)S(1)} %get-tuple-element.31), channel_id=1, source_target_pairs={{0,1},{1,0},{2,3},{3,2},{4,5},{5,4},{6,7},{7,6},{8,9},{9,8},{10,11... | collective-permute-start | bytes 159752 | tf_op jit(solution)/shard_map/ppermute | solution.py:371
  28.9 0.0 collective-permute-done.8.refs_1_
  28.9 0.0 collective-permute-done.9.refs_2_
  28.9 4.6 %stack1.1 = (s16[208,128]{1,0:T(8,128)(2,1)S(1)}, s16[208,128]{1,0:T(8,128)(2,1)S(1)}, s16[208,128]{1,0:T(8,128)(2,1)S(1)}, s16[208,128]{1,0:T(8,128)(2,1)S(1)}) custom-call(bf16[128,2048]{1,0:T(8,128)(2,1)S(1)} %whiten.1.refs_0_.refs_1_, bf16[128,2048]{1,0:T(8,128)(2,1)S(1)} %collective-permute-done.8.refs_1_, ...), custom_call_target="tpu_custom_call" | custom-call | flops 2147483648 | bytes 3145728 | tf_op jit(solution)/shard_map/stack1/pallas_call | solution.py:292
  33.5 2.2 %collective-permute-start.10 = (s16[208,128]{1,0:T(8,128)(2,1)S(1)}, s16[208,128]{1,0:T(8,128)(2,1)S(1)}, u32[]{:S(2)}, u32[]{:S(2)}) collective-permute-start(s16[208,128]{1,0:T(8,128)(2,1)S(1)} %get-tuple-element.34), channel_id=1, source_target_pairs={{0,3},{1,2},{2,1},{3,0},{4,7},{5,6},{6,5},{7,4},{8,11},{9,10},{10,... | collective-permute-start | bytes 159752 | tf_op jit(solution)/shard_map/ppermute | solution.py:371
  35.7 0.0 collective-permute-start.11
  35.7 0.0 collective-permute-done.4.refs_1_
  35.7 2.3 %collective-permute-start.12 = (s16[208,128]{1,0:T(8,128)(2,1)S(1)}, s16[208,128]{1,0:T(8,128)(2,1)S(1)}, u32[]{:S(2)}, u32[]{:S(2)}) collective-permute-start(s16[208,128]{1,0:T(8,128)(2,1)S(1)} %get-tuple-element.36), channel_id=1, source_target_pairs={{0,1},{1,0},{2,3},{3,2},{4,5},{5,4},{6,7},{7,6},{8,9},{9,8},{10,11... | collective-permute-start | bytes 159752 | tf_op jit(solution)/shard_map/ppermute | solution.py:371
  38.0 0.0 collective-permute-done.5.refs_2_
  38.0 0.0 collective-permute-done.6.refs_3_
  38.0 0.0 copy-start.3
  38.0 0.5 %finish2.1 = (f32[64,128]{1,0:T(8,128)S(1)}, f32[64,128]{1,0:T(8,128)S(1)}) custom-call(s16[208,128]{1,0:T(8,128)(2,1)S(1)} %get-tuple-element.28.refs_0_, s16[208,128]{1,0:T(8,128)(2,1)S(1)} %collective-permute-done.4.refs_1_, s16[208,128]{1,0:T(8,128)(2,1)S(1)} %collective-permute-done.5.refs_2_, s16[208,128]{1,0:T(8,128)(2,1)S(1)} %collective-permute-done.6.refs_3_), custom_call_target="tpu_custom_call" | custom-call | flops 4194304 | bytes 262144 | tf_op jit(solution)/shard_map/finish2/pallas_call | solution.py:359
  38.5 3.3 %collective-permute-start.7 = (f32[64,128]{1,0:T(8,128)S(1)}, f32[64,128]{1,0:T(8,128)S(1)}, u32[]{:S(2)}, u32[]{:S(2)}) collective-permute-start(f32[64,128]{1,0:T(8,128)S(1)} %get-tuple-element.32), channel_id=1, source_target_pairs={{0,11},{1,10},{2,9},{3,8},{4,15},{5,14},{6,13},{7,12},{8,19},{9,18... | collective-permute-start | bytes 98312 | tf_op jit(solution)/shard_map/ppermute | solution.py:394
  41.8 0.0 copy-done.3
  41.8 0.0 collective-permute-done.10.refs_1_
  41.8 0.0 collective-permute-done.11.refs_2_
  41.8 0.0 collective-permute-done.12.refs_3_
  41.8 0.5 %finish1.1 = (f32[64,128]{1,0:T(8,128)S(1)}, f32[64,128]{1,0:T(8,128)S(1)}) custom-call(s16[208,128]{1,0:T(8,128)(2,1)S(1)} %get-tuple-element.33.refs_0_, s16[208,128]{1,0:T(8,128)(2,1)S(1)} %collective-permute-done.10.refs_1_, s16[208,128]{1,0:T(8,128)(2,1)S(1)} %collective-permute-done.11.refs_2_, s16[208,128]{1,0:T(8,128)(2,1)S(1)} %collective-permute-done.12.refs_3_), custom_call_target="tpu_custom_call" | custom-call | flops 4194304 | bytes 262144 | tf_op jit(solution)/shard_map/finish1/pallas_call | solution.py:359
  42.4 0.3 collective-permute-start.13
  42.7 3.4 %collective-permute-done.7 = f32[64,128]{1,0:T(8,128)S(1)} collective-permute-done((f32[64,128]{1,0:T(8,128)S(1)}, f32[64,128]{1,0:T(8,128)S(1)}, u32[]{:S(2)}, u32[]{:S(2)}) %collective-permute-start.7) | collective-permute-done | bytes 32800 | tf_op jit(solution)/shard_map/ppermute | solution.py:394
  46.1 3.3 %collective-permute-done.13 = f32[64,128]{1,0:T(8,128)S(1)} collective-permute-done((f32[64,128]{1,0:T(8,128)S(1)}, f32[64,128]{1,0:T(8,128)S(1)}, u32[]{:S(2)}, u32[]{:S(2)}) %collective-permute-start.13) | collective-permute-done | bytes 32800 | tf_op jit(solution)/shard_map/ppermute | solution.py:394
  49.4 0.8 %broadcast_multiply_fusion.1 = f32[8,5,8,128]{3,2,1,0:T(8,128)} fusion(f32[8,5,8,128]{3,2,1,0:T(8,128)S(1)} %bitcast_dynamic-update-slice_fusion, f32[8,5,8]{2,1,0:T(8,128)S(1)} %copy.16), kind=kLoop, calls=%fused_computation.2 | loop fusion | flops 40960 | bytes 328960 | tf_op jit(solution)/shard_map/mul | solution.py:404
  (8 shorter events, 0.0 us)
Async XLA Ops:
  0.0 1.6 %copy-start.2 = (bf16[8,256,256]{2,1,0:T(8,128)(2,1)S(1)}, bf16[8,256,256]{2,1,0:T(8,128)(2,1)}, u32[]{:S(2)}) copy-start(bf16[8,256,256]{2,1,0:T(8,128)(2,1)} %constant.8.clone) | copy-start | bytes 3145732
  0.0 1.6 %copy-start.4 = (s32[8,16]{1,0:T(8,128)S(1)}, s32[8,16]{1,0:T(8,128)}, u32[]{:S(2)}) copy-start(s32[8,16]{1,0:T(8,128)} %param.11) | copy-start | bytes 1540
  1.7 5.2 %copy-start = (bf16[1024,512]{1,0:T(8,128)(2,1)S(1)}, bf16[1024,512]{1,0:T(8,128)(2,1)}, u32[]{:S(2)}) copy-start(bf16[1024,512]{1,0:T(8,128)(2,1)} %constant.9.clone.refs_2_.refs_3_) | copy-start | bytes 3145732
  1.7 5.2 %copy-start.1 = (bf16[512,256]{1,0:T(8,128)(2,1)S(1)}, bf16[512,256]{1,0:T(8,128)(2,1)}, u32[]{:S(2)}) copy-start(bf16[512,256]{1,0:T(8,128)(2,1)} %constant.10.clone.refs_3_.refs_4_) | copy-start | bytes 786436
  2.9 17.3 %collective-permute-start = (bf16[128,2048]{1,0:T(8,128)(2,1)S(1)}, bf16[128,2048]{1,0:T(8,128)(2,1)S(1)}, u32[]{:S(2)}, u32[]{:S(2)}) collective-permute-start(bf16[128,2048]{1,0:T(8,128)(2,1)S(1)} %whiten.1.refs_0_.refs_1_), channel_id=1, source_target_pairs={{8,0},{12,4},{16,8},{20,12},{24,16},{28,20},{0,24},{4,28},{9,1},{1... | collective-permute-start | bytes 1572872 | tf_op jit(solution)/shard_map/ppermute | solution.py:380
  11.1 6.6 %collective-permute-start.1 = (s16[208,128]{1,0:T(8,128)(2,1)S(1)}, s16[208,128]{1,0:T(8,128)(2,1)S(1)}, u32[]{:S(2)}, u32[]{:S(2)}) collective-permute-start(s16[208,128]{1,0:T(8,128)(2,1)S(1)} %get-tuple-element.24), channel_id=1, source_target_pairs={{0,3},{1,2},{2,1},{3,0},{4,7},{5,6},{6,5},{7,4},{8,11},{9,10},{10,... | collective-permute-start | bytes 159752 | tf_op jit(solution)/shard_map/ppermute | solution.py:371
  14.8 5.0 %collective-permute-start.2 = (s16[208,128]{1,0:T(8,128)(2,1)S(1)}, s16[208,128]{1,0:T(8,128)(2,1)S(1)}, u32[]{:S(2)}, u32[]{:S(2)}) collective-permute-start(s16[208,128]{1,0:T(8,128)(2,1)S(1)} %get-tuple-element.25), channel_id=1, source_target_pairs={{0,2},{1,3},{2,0},{3,1},{4,6},{5,7},{6,4},{7,5},{8,10},{9,11},{10,... | collective-permute-start | bytes 159752 | tf_op jit(solution)/shard_map/ppermute | solution.py:371
  14.8 5.0 %collective-permute-start.3 = (s16[208,128]{1,0:T(8,128)(2,1)S(1)}, s16[208,128]{1,0:T(8,128)(2,1)S(1)}, u32[]{:S(2)}, u32[]{:S(2)}) collective-permute-start(s16[208,128]{1,0:T(8,128)(2,1)S(1)} %get-tuple-element.26), channel_id=1, source_target_pairs={{0,1},{1,0},{2,3},{3,2},{4,5},{5,4},{6,7},{7,6},{8,9},{9,8},{10,11... | collective-permute-start | bytes 159752 | tf_op jit(solution)/shard_map/ppermute | solution.py:371
  15.5 13.4 %collective-permute-start.8 = (bf16[128,2048]{1,0:T(8,128)(2,1)S(1)}, bf16[128,2048]{1,0:T(8,128)(2,1)S(1)}, u32[]{:S(2)}, u32[]{:S(2)}) collective-permute-start(bf16[128,2048]{1,0:T(8,128)(2,1)S(1)} %whiten.1.refs_0_.refs_1_), channel_id=1, source_target_pairs={{4,0},{0,4},{12,8},{8,12},{20,16},{16,20},{28,24},{24,28},{5,1},{1... | collective-permute-start | bytes 1572872 | tf_op jit(solution)/shard_map/ppermute | solution.py:381
  20.2 8.7 %collective-permute-start.9 = (bf16[128,2048]{1,0:T(8,128)(2,1)S(1)}, bf16[128,2048]{1,0:T(8,128)(2,1)S(1)}, u32[]{:S(2)}, u32[]{:S(2)}) collective-permute-start(bf16[128,2048]{1,0:T(8,128)(2,1)S(1)} %collective-permute-done.refs_1_), channel_id=1, source_target_pairs={{4,0},{0,4},{12,8},{8,12},{20,16},{16,20},{28,24},{24,28},{5,1},{1... | collective-permute-start | bytes 1572872 | tf_op jit(solution)/shard_map/ppermute | solution.py:385
  24.5 11.2 %collective-permute-start.4 = (s16[208,128]{1,0:T(8,128)(2,1)S(1)}, s16[208,128]{1,0:T(8,128)(2,1)S(1)}, u32[]{:S(2)}, u32[]{:S(2)}) collective-permute-start(s16[208,128]{1,0:T(8,128)(2,1)S(1)} %get-tuple-element.29), channel_id=1, source_target_pairs={{0,3},{1,2},{2,1},{3,0},{4,7},{5,6},{6,5},{7,4},{8,11},{9,10},{10,... | collective-permute-start | bytes 159752 | tf_op jit(solution)/shard_map/ppermute | solution.py:371
  26.6 11.3 %collective-permute-start.5 = (s16[208,128]{1,0:T(8,128)(2,1)S(1)}, s16[208,128]{1,0:T(8,128)(2,1)S(1)}, u32[]{:S(2)}, u32[]{:S(2)}) collective-permute-start(s16[208,128]{1,0:T(8,128)(2,1)S(1)} %get-tuple-element.30), channel_id=1, source_target_pairs={{0,2},{1,3},{2,0},{3,1},{4,6},{5,7},{6,4},{7,5},{8,10},{9,11},{10,... | collective-permute-start | bytes 159752 | tf_op jit(solution)/shard_map/ppermute | solution.py:371
  26.7 11.3 %collective-permute-start.6 = (s16[208,128]{1,0:T(8,128)(2,1)S(1)}, s16[208,128]{1,0:T(8,128)(2,1)S(1)}, u32[]{:S(2)}, u32[]{:S(2)}) collective-permute-start(s16[208,128]{1,0:T(8,128)(2,1)S(1)} %get-tuple-element.31), channel_id=1, source_target_pairs={{0,1},{1,0},{2,3},{3,2},{4,5},{5,4},{6,7},{7,6},{8,9},{9,8},{10,11... | collective-permute-start | bytes 159752 | tf_op jit(solution)/shard_map/ppermute | solution.py:371
  33.5 8.3 %collective-permute-start.10 = (s16[208,128]{1,0:T(8,128)(2,1)S(1)}, s16[208,128]{1,0:T(8,128)(2,1)S(1)}, u32[]{:S(2)}, u32[]{:S(2)}) collective-permute-start(s16[208,128]{1,0:T(8,128)(2,1)S(1)} %get-tuple-element.34), channel_id=1, source_target_pairs={{0,3},{1,2},{2,1},{3,0},{4,7},{5,6},{6,5},{7,4},{8,11},{9,10},{10,... | collective-permute-start | bytes 159752 | tf_op jit(solution)/shard_map/ppermute | solution.py:371
  35.7 6.1 %collective-permute-start.11 = (s16[208,128]{1,0:T(8,128)(2,1)S(1)}, s16[208,128]{1,0:T(8,128)(2,1)S(1)}, u32[]{:S(2)}, u32[]{:S(2)}) collective-permute-start(s16[208,128]{1,0:T(8,128)(2,1)S(1)} %get-tuple-element.35), channel_id=1, source_target_pairs={{0,2},{1,3},{2,0},{3,1},{4,6},{5,7},{6,4},{7,5},{8,10},{9,11},{10,... | collective-permute-start | bytes 159752 | tf_op jit(solution)/shard_map/ppermute | solution.py:371
  35.7 6.2 %collective-permute-start.12 = (s16[208,128]{1,0:T(8,128)(2,1)S(1)}, s16[208,128]{1,0:T(8,128)(2,1)S(1)}, u32[]{:S(2)}, u32[]{:S(2)}) collective-permute-start(s16[208,128]{1,0:T(8,128)(2,1)S(1)} %get-tuple-element.36), channel_id=1, source_target_pairs={{0,1},{1,0},{2,3},{3,2},{4,5},{5,4},{6,7},{7,6},{8,9},{9,8},{10,11... | collective-permute-start | bytes 159752 | tf_op jit(solution)/shard_map/ppermute | solution.py:371
  38.0 3.8 %copy-start.3 = (s32[8,5,8]{2,0,1:T(8,128)S(1)}, s32[8,5,8]{2,0,1:T(8,128)}, u32[]{:S(2)}) copy-start(s32[8,5,8]{2,0,1:T(8,128)} %param.12) | copy-start | bytes 3844
  38.5 7.5 %collective-permute-start.7 = (f32[64,128]{1,0:T(8,128)S(1)}, f32[64,128]{1,0:T(8,128)S(1)}, u32[]{:S(2)}, u32[]{:S(2)}) collective-permute-start(f32[64,128]{1,0:T(8,128)S(1)} %get-tuple-element.32), channel_id=1, source_target_pairs={{0,11},{1,10},{2,9},{3,8},{4,15},{5,14},{6,13},{7,12},{8,19},{9,18... | collective-permute-start | bytes 98312 | tf_op jit(solution)/shard_map/ppermute | solution.py:394
  42.4 6.9 %collective-permute-start.13 = (f32[64,128]{1,0:T(8,128)S(1)}, f32[64,128]{1,0:T(8,128)S(1)}, u32[]{:S(2)}, u32[]{:S(2)}) collective-permute-start(f32[64,128]{1,0:T(8,128)S(1)} %get-tuple-element.37), channel_id=1, source_target_pairs={{0,7},{1,6},{2,5},{3,4},{4,11},{5,10},{6,9},{7,8},{8,15},{9,14},{1... | collective-permute-start | bytes 98312 | tf_op jit(solution)/shard_map/ppermute | solution.py:394

commit v4 on v3

--- a/solution.py
+++ b/solution.py
@@ -380,8 +380,7 @@
     second = lax.ppermute(white, "sta", [((i + 2) % blocks, i) for i in range(blocks)])
     beside = lax.ppermute(white, "sta", [(i ^ 1, i) for i in range(blocks)])
     own_sums = exchange(unit(stations, parts, white, [white], "stack0"))
-    (middle,) = finish(stations, windows, own_sums, False, "finish0")
-    second, middle = lax.optimization_barrier((second, middle))
+    second, *own_sums = lax.optimization_barrier((second, *own_sums))
     handed = lax.ppermute(second, "sta", [(i ^ 1, i) for i in range(blocks)])
     far_sums = exchange(unit(stations, parts, white, [second], "stack2"))
     near_sums = exchange(unit(stations, parts, white, [beside, handed], "stack1"))
@@ -395,6 +394,7 @@
 
     far, far_back = finish(stations, windows, far_sums, True, "finish2")
     far_back = returned(far_back, 2)
+    (middle,) = finish(stations, windows, own_sums, False, "finish0")
     near, near_back = finish(stations, windows, near_sums, True, "finish1")
     near_back = returned(near_back, 1)
     wide = LAGS // parts

time: 50.3 us -> 50.7 us (level)
  no operation moved by 1% of the time
where the time goes in v4:
time: 50.7 us; the launch traced here: 50.6 us
  starting transfers between devices  21 us (41%)
  Pallas kernels  15.6 us (31%)
  waiting for transfers between devices  11.2 us (22%)
  other arithmetic  2.44 us (5%)
    ppermute x9, starting transfers between devices, exchange(): lax.ppermute(sums[d], 'win', [(i, i ^ d) for i in range(parts)])  13.4 us
    pallas_call x3, Pallas kernels, unit(): pl.pallas_call(functools.partial(unit_kernel, stations, windows, parts, c...  13 us
    ppermute x2, waiting for transfers between devices, returned(): return lax.ppermute(value, ('sta', 'win'), route)  6.93 us
    ppermute x9, waiting for transfers between devices, exchange(): lax.ppermute(sums[d], 'win', [(i, i ^ d) for i in range(parts)])  4.27 us
    ppermute x1, starting transfers between devices, local(): lax.ppermute(white, 'sta', [((i + 2) % blocks, i) for i in range(blocks)])  3.95 us
    ppermute x2, starting transfers between devices, returned(): return lax.ppermute(value, ('sta', 'win'), route)  3.73 us
    convert_element_type x1, other arithmetic, forward(): signs = jnp.sign(traces.reshape(rows, samples)).astype(jnp.bfloat16)  1.58 us
    pallas_call x3, Pallas kernels, finish(): pl.pallas_call(functools.partial(finish_kernel, stations, windows, parts,...  1.49 us
  transfers between devices with their start and end apart: 14, of which 4 were waited for; matrix products, arithmetic and copies ran while one was open for 0% of the time, Pallas kernels for 29%

profile of v4, /device:TPU:0, one launch (start us, length us, event | category | flops | bytes accessed | tf_op | source)
XLA Modules:
  0.0 50.6 jit_solution(2765187817243650047)
XLA Ops:
  0.0 0.0 copy-start.2
  0.0 0.0 copy-start.4
  0.0 1.6 %sign_convert_fusion = bf16[8,16,2048]{2,1,0:T(8,128)(2,1)S(1)} fusion(f32[8,16,2048]{2,1,0:T(8,128)} %param.10), kind=kLoop, calls=%fused_computation | loop fusion | flops 524288 | bytes 1572864 | tf_op jit(solution)/shard_map/convert_element_type | solution.py:145
  1.6 0.0 copy-done.4
  1.6 0.0 copy-done.2
  1.6 0.1 broadcast_multiply_fusion.table
  1.7 0.0 copy-start
  1.7 0.0 copy-start.1
  1.7 1.2 %whiten.1.refs_0_.refs_1_ = bf16[128,2048]{1,0:T(8,128)(2,1)S(1)} custom-call(bf16[128,2048]{1,0:T(8,128)(2,1)S(1)} %bitcast.21, f32[8,16]{1,0:T(8,128)S(1)} %convert_element_type.13.flags, bf16[8,256,256]{2,1,0:T(8,128)(2,1)S(1)} %broadcast_multiply_fusion.table), custom_call_target="tpu_custom_call" | custom-call | flops 402653184 | bytes 4194304 | tf_op jit(solution)/shard_map/whiten/pallas_call | solution.py:147
  2.9 3.9 %collective-permute-start = (bf16[128,2048]{1,0:T(8,128)(2,1)S(1)}, bf16[128,2048]{1,0:T(8,128)(2,1)S(1)}, u32[]{:S(2)}, u32[]{:S(2)}) collective-permute-start(bf16[128,2048]{1,0:T(8,128)(2,1)S(1)} %whiten.1.refs_0_.refs_1_), channel_id=1, source_target_pairs={{8,0},{12,4},{16,8},{20,12},{24,16},{28,20},{0,24},{4,28},{9,1},{1... | collective-permute-start | bytes 1572872 | tf_op jit(solution)/shard_map/ppermute | solution.py:380
  6.9 0.0 copy-done
  6.9 0.0 copy-done.1
  6.9 4.2 %stack0.1 = (s16[208,128]{1,0:T(8,128)(2,1)S(1)}, s16[208,128]{1,0:T(8,128)(2,1)S(1)}, s16[208,128]{1,0:T(8,128)(2,1)S(1)}, s16[208,128]{1,0:T(8,128)(2,1)S(1)}) custom-call(bf16[128,2048]{1,0:T(8,128)(2,1)S(1)} %whiten.1.refs_0_.refs_1_, bf16[128,2048]{1,0:T(8,128)(2,1)S(1)} %whiten.1.refs_0_.refs_1_, bf16[1024,512]{1,0:T(8,128)(2,1)S(1)} %copy-done, ...), custom_call_target="tpu_custom_call" | custom-call | flops 2147483648 | bytes 3145728 | tf_op jit(solution)/shard_map/stack0/pallas_call | solution.py:292
  11.1 3.7 %collective-permute-start.1 = (s16[208,128]{1,0:T(8,128)(2,1)S(1)}, s16[208,128]{1,0:T(8,128)(2,1)S(1)}, u32[]{:S(2)}, u32[]{:S(2)}) collective-permute-start(s16[208,128]{1,0:T(8,128)(2,1)S(1)} %get-tuple-element.27), channel_id=1, source_target_pairs={{0,3},{1,2},{2,1},{3,0},{4,7},{5,6},{6,5},{7,4},{8,11},{9,10},{10,... | collective-permute-start | bytes 159752 | tf_op jit(solution)/shard_map/ppermute | solution.py:371
  14.8 0.0 collective-permute-start.2
  14.8 0.8 %collective-permute-start.3 = (s16[208,128]{1,0:T(8,128)(2,1)S(1)}, s16[208,128]{1,0:T(8,128)(2,1)S(1)}, u32[]{:S(2)}, u32[]{:S(2)}) collective-permute-start(s16[208,128]{1,0:T(8,128)(2,1)S(1)} %get-tuple-element.29), channel_id=1, source_target_pairs={{0,1},{1,0},{2,3},{3,2},{4,5},{5,4},{6,7},{7,6},{8,9},{9,8},{10,11... | collective-permute-start | bytes 159752 | tf_op jit(solution)/shard_map/ppermute | solution.py:371
  15.5 0.0 collective-permute-start.8
  15.5 2.2 %collective-permute-done.1.refs_1_ = s16[208,128]{1,0:T(8,128)(2,1)S(1)} collective-permute-done((s16[208,128]{1,0:T(8,128)(2,1)S(1)}, s16[208,128]{1,0:T(8,128)(2,1)S(1)}, u32[]{:S(2)}, u32[]{:S(2)}) %collective-permute-start.1) | collective-permute-done | bytes 53280 | tf_op jit(solution)/shard_map/ppermute | solution.py:371
  17.7 2.1 %collective-permute-done.2.refs_2_ = s16[208,128]{1,0:T(8,128)(2,1)S(1)} collective-permute-done((s16[208,128]{1,0:T(8,128)(2,1)S(1)}, s16[208,128]{1,0:T(8,128)(2,1)S(1)}, u32[]{:S(2)}, u32[]{:S(2)}) %collective-permute-start.2) | collective-permute-done | bytes 53280 | tf_op jit(solution)/shard_map/ppermute | solution.py:371
  19.8 0.0 collective-permute-done.3.refs_3_
  19.8 0.0 collective-permute-done.refs_1_
  19.8 0.0 collective-permute-start.9
  19.8 4.2 %stack2.1 = (s16[208,128]{1,0:T(8,128)(2,1)S(1)}, s16[208,128]{1,0:T(8,128)(2,1)S(1)}, s16[208,128]{1,0:T(8,128)(2,1)S(1)}, s16[208,128]{1,0:T(8,128)(2,1)S(1)}) custom-call(bf16[128,2048]{1,0:T(8,128)(2,1)S(1)} %whiten.1.refs_0_.refs_1_, bf16[128,2048]{1,0:T(8,128)(2,1)S(1)} %collective-permute-done.refs_1_, bf16[1024,512]{1,0:T(8,128)(2,1)S(1)} %copy-done, ...), custom_call_target="tpu_custom_call" | custom-call | flops 2147483648 | bytes 3145728 | tf_op jit(solution)/shard_map/stack2/pallas_call | solution.py:292
  24.0 2.2 %collective-permute-start.4 = (s16[208,128]{1,0:T(8,128)(2,1)S(1)}, s16[208,128]{1,0:T(8,128)(2,1)S(1)}, u32[]{:S(2)}, u32[]{:S(2)}) collective-permute-start(s16[208,128]{1,0:T(8,128)(2,1)S(1)} %get-tuple-element.32), channel_id=1, source_target_pairs={{0,3},{1,2},{2,1},{3,0},{4,7},{5,6},{6,5},{7,4},{8,11},{9,10},{10,... | collective-permute-start | bytes 159752 | tf_op jit(solution)/shard_map/ppermute | solution.py:371
  26.2 0.0 collective-permute-start.5
  26.2 2.3 %collective-permute-start.6 = (s16[208,128]{1,0:T(8,128)(2,1)S(1)}, s16[208,128]{1,0:T(8,128)(2,1)S(1)}, u32[]{:S(2)}, u32[]{:S(2)}) collective-permute-start(s16[208,128]{1,0:T(8,128)(2,1)S(1)} %get-tuple-element.34), channel_id=1, source_target_pairs={{0,1},{1,0},{2,3},{3,2},{4,5},{5,4},{6,7},{7,6},{8,9},{9,8},{10,11... | collective-permute-start | bytes 159752 | tf_op jit(solution)/shard_map/ppermute | solution.py:371
  28.5 0.0 collective-permute-done.8.refs_1_
  28.5 0.0 collective-permute-done.9.refs_2_
  28.5 4.6 %stack1.1 = (s16[208,128]{1,0:T(8,128)(2,1)S(1)}, s16[208,128]{1,0:T(8,128)(2,1)S(1)}, s16[208,128]{1,0:T(8,128)(2,1)S(1)}, s16[208,128]{1,0:T(8,128)(2,1)S(1)}) custom-call(bf16[128,2048]{1,0:T(8,128)(2,1)S(1)} %whiten.1.refs_0_.refs_1_, bf16[128,2048]{1,0:T(8,128)(2,1)S(1)} %collective-permute-done.8.refs_1_, ...), custom_call_target="tpu_custom_call" | custom-call | flops 2147483648 | bytes 3145728 | tf_op jit(solution)/shard_map/stack1/pallas_call | solution.py:292
  33.1 2.2 %collective-permute-start.10 = (s16[208,128]{1,0:T(8,128)(2,1)S(1)}, s16[208,128]{1,0:T(8,128)(2,1)S(1)}, u32[]{:S(2)}, u32[]{:S(2)}) collective-permute-start(s16[208,128]{1,0:T(8,128)(2,1)S(1)} %get-tuple-element.37), channel_id=1, source_target_pairs={{0,3},{1,2},{2,1},{3,0},{4,7},{5,6},{6,5},{7,4},{8,11},{9,10},{10,... | collective-permute-start | bytes 159752 | tf_op jit(solution)/shard_map/ppermute | solution.py:371
  35.2 0.0 collective-permute-start.11
  35.2 0.0 collective-permute-done.4.refs_1_
  35.2 2.3 %collective-permute-start.12 = (s16[208,128]{1,0:T(8,128)(2,1)S(1)}, s16[208,128]{1,0:T(8,128)(2,1)S(1)}, u32[]{:S(2)}, u32[]{:S(2)}) collective-permute-start(s16[208,128]{1,0:T(8,128)(2,1)S(1)} %get-tuple-element.39), channel_id=1, source_target_pairs={{0,1},{1,0},{2,3},{3,2},{4,5},{5,4},{6,7},{7,6},{8,9},{9,8},{10,11... | collective-permute-start | bytes 159752 | tf_op jit(solution)/shard_map/ppermute | solution.py:371
  37.5 0.0 collective-permute-done.5.refs_2_
  37.5 0.0 collective-permute-done.6.refs_3_
  37.5 0.0 copy-start.3
  37.5 0.5 %finish2.1 = (f32[64,128]{1,0:T(8,128)S(1)}, f32[64,128]{1,0:T(8,128)S(1)}) custom-call(s16[208,128]{1,0:T(8,128)(2,1)S(1)} %get-tuple-element.31.refs_0_, s16[208,128]{1,0:T(8,128)(2,1)S(1)} %collective-permute-done.4.refs_1_, s16[208,128]{1,0:T(8,128)(2,1)S(1)} %collective-permute-done.5.refs_2_, s16[208,128]{1,0:T(8,128)(2,1)S(1)} %collective-permute-done.6.refs_3_), custom_call_target="tpu_custom_call" | custom-call | flops 4194304 | bytes 262144 | tf_op jit(solution)/shard_map/finish2/pallas_call | solution.py:359
  38.1 3.7 %collective-permute-start.7 = (f32[64,128]{1,0:T(8,128)S(1)}, f32[64,128]{1,0:T(8,128)S(1)}, u32[]{:S(2)}, u32[]{:S(2)}) collective-permute-start(f32[64,128]{1,0:T(8,128)S(1)} %get-tuple-element.35), channel_id=1, source_target_pairs={{0,11},{1,10},{2,9},{3,8},{4,15},{5,14},{6,13},{7,12},{8,19},{9,18... | collective-permute-start | bytes 98312 | tf_op jit(solution)/shard_map/ppermute | solution.py:393
  41.8 0.0 copy-done.3
  41.8 0.4 finish0.1
  42.2 0.0 collective-permute-done.10.refs_1_
  42.2 0.0 collective-permute-done.11.refs_2_
  42.2 0.0 collective-permute-done.12.refs_3_
  42.3 0.5 %finish1.1 = (f32[64,128]{1,0:T(8,128)S(1)}, f32[64,128]{1,0:T(8,128)S(1)}) custom-call(s16[208,128]{1,0:T(8,128)(2,1)S(1)} %get-tuple-element.36.refs_0_, s16[208,128]{1,0:T(8,128)(2,1)S(1)} %collective-permute-done.10.refs_1_, s16[208,128]{1,0:T(8,128)(2,1)S(1)} %collective-permute-done.11.refs_2_, s16[208,128]{1,0:T(8,128)(2,1)S(1)} %collective-permute-done.12.refs_3_), custom_call_target="tpu_custom_call" | custom-call | flops 4194304 | bytes 262144 | tf_op jit(solution)/shard_map/finish1/pallas_call | solution.py:359
  42.8 0.0 collective-permute-start.13
  42.8 2.8 %collective-permute-done.7 = f32[64,128]{1,0:T(8,128)S(1)} collective-permute-done((f32[64,128]{1,0:T(8,128)S(1)}, f32[64,128]{1,0:T(8,128)S(1)}, u32[]{:S(2)}, u32[]{:S(2)}) %collective-permute-start.7) | collective-permute-done | bytes 32800 | tf_op jit(solution)/shard_map/ppermute | solution.py:393
  45.6 4.2 %collective-permute-done.13 = f32[64,128]{1,0:T(8,128)S(1)} collective-permute-done((f32[64,128]{1,0:T(8,128)S(1)}, f32[64,128]{1,0:T(8,128)S(1)}, u32[]{:S(2)}, u32[]{:S(2)}) %collective-permute-start.13) | collective-permute-done | bytes 32800 | tf_op jit(solution)/shard_map/ppermute | solution.py:393
  49.8 0.8 %broadcast_multiply_fusion.1 = f32[8,5,8,128]{3,2,1,0:T(8,128)} fusion(f32[8,5,8,128]{3,2,1,0:T(8,128)S(1)} %bitcast_dynamic-update-slice_fusion, f32[8,5,8]{2,1,0:T(8,128)S(1)} %copy.16), kind=kLoop, calls=%fused_computation.2 | loop fusion | flops 40960 | bytes 328960 | tf_op jit(solution)/shard_map/mul | solution.py:404
  (8 shorter events, 0.0 us)
Async XLA Ops:
  0.0 1.6 %copy-start.2 = (bf16[8,256,256]{2,1,0:T(8,128)(2,1)S(1)}, bf16[8,256,256]{2,1,0:T(8,128)(2,1)}, u32[]{:S(2)}) copy-start(bf16[8,256,256]{2,1,0:T(8,128)(2,1)} %constant.8.clone) | copy-start | bytes 3145732
  0.0 1.6 %copy-start.4 = (s32[8,16]{1,0:T(8,128)S(1)}, s32[8,16]{1,0:T(8,128)}, u32[]{:S(2)}) copy-start(s32[8,16]{1,0:T(8,128)} %param.11) | copy-start | bytes 1540
  1.7 5.2 %copy-start = (bf16[1024,512]{1,0:T(8,128)(2,1)S(1)}, bf16[1024,512]{1,0:T(8,128)(2,1)}, u32[]{:S(2)}) copy-start(bf16[1024,512]{1,0:T(8,128)(2,1)} %constant.9.clone.refs_2_.refs_3_) | copy-start | bytes 3145732
  1.7 5.2 %copy-start.1 = (bf16[512,256]{1,0:T(8,128)(2,1)S(1)}, bf16[512,256]{1,0:T(8,128)(2,1)}, u32[]{:S(2)}) copy-start(bf16[512,256]{1,0:T(8,128)(2,1)} %constant.10.clone.refs_3_.refs_4_) | copy-start | bytes 786436
  2.9 16.9 %collective-permute-start = (bf16[128,2048]{1,0:T(8,128)(2,1)S(1)}, bf16[128,2048]{1,0:T(8,128)(2,1)S(1)}, u32[]{:S(2)}, u32[]{:S(2)}) collective-permute-start(bf16[128,2048]{1,0:T(8,128)(2,1)S(1)} %whiten.1.refs_0_.refs_1_), channel_id=1, source_target_pairs={{8,0},{12,4},{16,8},{20,12},{24,16},{28,20},{0,24},{4,28},{9,1},{1... | collective-permute-start | bytes 1572872 | tf_op jit(solution)/shard_map/ppermute | solution.py:380
  11.1 6.6 %collective-permute-start.1 = (s16[208,128]{1,0:T(8,128)(2,1)S(1)}, s16[208,128]{1,0:T(8,128)(2,1)S(1)}, u32[]{:S(2)}, u32[]{:S(2)}) collective-permute-start(s16[208,128]{1,0:T(8,128)(2,1)S(1)} %get-tuple-element.27), channel_id=1, source_target_pairs={{0,3},{1,2},{2,1},{3,0},{4,7},{5,6},{6,5},{7,4},{8,11},{9,10},{10,... | collective-permute-start | bytes 159752 | tf_op jit(solution)/shard_map/ppermute | solution.py:371
  14.8 5.0 %collective-permute-start.2 = (s16[208,128]{1,0:T(8,128)(2,1)S(1)}, s16[208,128]{1,0:T(8,128)(2,1)S(1)}, u32[]{:S(2)}, u32[]{:S(2)}) collective-permute-start(s16[208,128]{1,0:T(8,128)(2,1)S(1)} %get-tuple-element.28), channel_id=1, source_target_pairs={{0,2},{1,3},{2,0},{3,1},{4,6},{5,7},{6,4},{7,5},{8,10},{9,11},{10,... | collective-permute-start | bytes 159752 | tf_op jit(solution)/shard_map/ppermute | solution.py:371
  14.8 5.0 %collective-permute-start.3 = (s16[208,128]{1,0:T(8,128)(2,1)S(1)}, s16[208,128]{1,0:T(8,128)(2,1)S(1)}, u32[]{:S(2)}, u32[]{:S(2)}) collective-permute-start(s16[208,128]{1,0:T(8,128)(2,1)S(1)} %get-tuple-element.29), channel_id=1, source_target_pairs={{0,1},{1,0},{2,3},{3,2},{4,5},{5,4},{6,7},{7,6},{8,9},{9,8},{10,11... | collective-permute-start | bytes 159752 | tf_op jit(solution)/shard_map/ppermute | solution.py:371
  15.5 12.9 %collective-permute-start.8 = (bf16[128,2048]{1,0:T(8,128)(2,1)S(1)}, bf16[128,2048]{1,0:T(8,128)(2,1)S(1)}, u32[]{:S(2)}, u32[]{:S(2)}) collective-permute-start(bf16[128,2048]{1,0:T(8,128)(2,1)S(1)} %whiten.1.refs_0_.refs_1_), channel_id=1, source_target_pairs={{4,0},{0,4},{12,8},{8,12},{20,16},{16,20},{28,24},{24,28},{5,1},{1... | collective-permute-start | bytes 1572872 | tf_op jit(solution)/shard_map/ppermute | solution.py:381
  19.8 8.7 %collective-permute-start.9 = (bf16[128,2048]{1,0:T(8,128)(2,1)S(1)}, bf16[128,2048]{1,0:T(8,128)(2,1)S(1)}, u32[]{:S(2)}, u32[]{:S(2)}) collective-permute-start(bf16[128,2048]{1,0:T(8,128)(2,1)S(1)} %collective-permute-done.refs_1_), channel_id=1, source_target_pairs={{4,0},{0,4},{12,8},{8,12},{20,16},{16,20},{28,24},{24,28},{5,1},{1... | collective-permute-start | bytes 1572872 | tf_op jit(solution)/shard_map/ppermute | solution.py:384
  24.0 11.2 %collective-permute-start.4 = (s16[208,128]{1,0:T(8,128)(2,1)S(1)}, s16[208,128]{1,0:T(8,128)(2,1)S(1)}, u32[]{:S(2)}, u32[]{:S(2)}) collective-permute-start(s16[208,128]{1,0:T(8,128)(2,1)S(1)} %get-tuple-element.32), channel_id=1, source_target_pairs={{0,3},{1,2},{2,1},{3,0},{4,7},{5,6},{6,5},{7,4},{8,11},{9,10},{10,... | collective-permute-start | bytes 159752 | tf_op jit(solution)/shard_map/ppermute | solution.py:371
  26.2 11.3 %collective-permute-start.5 = (s16[208,128]{1,0:T(8,128)(2,1)S(1)}, s16[208,128]{1,0:T(8,128)(2,1)S(1)}, u32[]{:S(2)}, u32[]{:S(2)}) collective-permute-start(s16[208,128]{1,0:T(8,128)(2,1)S(1)} %get-tuple-element.33), channel_id=1, source_target_pairs={{0,2},{1,3},{2,0},{3,1},{4,6},{5,7},{6,4},{7,5},{8,10},{9,11},{10,... | collective-permute-start | bytes 159752 | tf_op jit(solution)/shard_map/ppermute | solution.py:371
  26.2 11.3 %collective-permute-start.6 = (s16[208,128]{1,0:T(8,128)(2,1)S(1)}, s16[208,128]{1,0:T(8,128)(2,1)S(1)}, u32[]{:S(2)}, u32[]{:S(2)}) collective-permute-start(s16[208,128]{1,0:T(8,128)(2,1)S(1)} %get-tuple-element.34), channel_id=1, source_target_pairs={{0,1},{1,0},{2,3},{3,2},{4,5},{5,4},{6,7},{7,6},{8,9},{9,8},{10,11... | collective-permute-start | bytes 159752 | tf_op jit(solution)/shard_map/ppermute | solution.py:371
  33.1 9.2 %collective-permute-start.10 = (s16[208,128]{1,0:T(8,128)(2,1)S(1)}, s16[208,128]{1,0:T(8,128)(2,1)S(1)}, u32[]{:S(2)}, u32[]{:S(2)}) collective-permute-start(s16[208,128]{1,0:T(8,128)(2,1)S(1)} %get-tuple-element.37), channel_id=1, source_target_pairs={{0,3},{1,2},{2,1},{3,0},{4,7},{5,6},{6,5},{7,4},{8,11},{9,10},{10,... | collective-permute-start | bytes 159752 | tf_op jit(solution)/shard_map/ppermute | solution.py:371
  35.2 7.0 %collective-permute-start.11 = (s16[208,128]{1,0:T(8,128)(2,1)S(1)}, s16[208,128]{1,0:T(8,128)(2,1)S(1)}, u32[]{:S(2)}, u32[]{:S(2)}) collective-permute-start(s16[208,128]{1,0:T(8,128)(2,1)S(1)} %get-tuple-element.38), channel_id=1, source_target_pairs={{0,2},{1,3},{2,0},{3,1},{4,6},{5,7},{6,4},{7,5},{8,10},{9,11},{10,... | collective-permute-start | bytes 159752 | tf_op jit(solution)/shard_map/ppermute | solution.py:371
  35.2 7.0 %collective-permute-start.12 = (s16[208,128]{1,0:T(8,128)(2,1)S(1)}, s16[208,128]{1,0:T(8,128)(2,1)S(1)}, u32[]{:S(2)}, u32[]{:S(2)}) collective-permute-start(s16[208,128]{1,0:T(8,128)(2,1)S(1)} %get-tuple-element.39), channel_id=1, source_target_pairs={{0,1},{1,0},{2,3},{3,2},{4,5},{5,4},{6,7},{7,6},{8,9},{9,8},{10,11... | collective-permute-start | bytes 159752 | tf_op jit(solution)/shard_map/ppermute | solution.py:371
  37.5 4.3 %copy-start.3 = (s32[8,5,8]{2,0,1:T(8,128)S(1)}, s32[8,5,8]{2,0,1:T(8,128)}, u32[]{:S(2)}) copy-start(s32[8,5,8]{2,0,1:T(8,128)} %param.12) | copy-start | bytes 3844
  38.1 7.5 %collective-permute-start.7 = (f32[64,128]{1,0:T(8,128)S(1)}, f32[64,128]{1,0:T(8,128)S(1)}, u32[]{:S(2)}, u32[]{:S(2)}) collective-permute-start(f32[64,128]{1,0:T(8,128)S(1)} %get-tuple-element.35), channel_id=1, source_target_pairs={{0,11},{1,10},{2,9},{3,8},{4,15},{5,14},{6,13},{7,12},{8,19},{9,18... | collective-permute-start | bytes 98312 | tf_op jit(solution)/shard_map/ppermute | solution.py:393
  42.8 6.9 %collective-permute-start.13 = (f32[64,128]{1,0:T(8,128)S(1)}, f32[64,128]{1,0:T(8,128)S(1)}, u32[]{:S(2)}, u32[]{:S(2)}) collective-permute-start(f32[64,128]{1,0:T(8,128)S(1)} %get-tuple-element.40), channel_id=1, source_target_pairs={{0,7},{1,6},{2,5},{3,4},{4,11},{5,10},{6,9},{7,8},{8,15},{9,14},{1... | collective-permute-start | bytes 98312 | tf_op jit(solution)/shard_map/ppermute | solution.py:393
